TPU v7x, 512 devices: a whole 4x4x16 slice. The times are simulated.
512 devices in a mesh: dp: 16 (over z), bal: 32 (over y, x, core).
Axes of the slice: x: 4, y: 4, z: 16, core: 2. Of those that a mesh axis runs over, the one named last changes fastest.
Arguments:
- pixels: bfloat16 [163840, 588], P(('dp', 'bal'))
- latent: bfloat16 [1792, 588], replicated
- quant_scale: float32 [1792], replicated, as said below
- embed_bias: float32 [1792], replicated, may hold values from -6 to 6
- ln_gain: float32 [1792], replicated, may hold values from 0.5 to 1.5
- ln_bias: float32 [1792], replicated, may hold values from -3 to 3
- qkv_weight: bfloat16 [1792, 2688], P(None, 'dp'), may hold values from -0.1875 to 0.1875
- cotangent: bfloat16 [131072, 896], P(('dp', 'bal')), may hold values from -6 to 6
- image_length: int32 [16, 128], P('dp'), may hold values from 0 to 192, as said below
- image_source: int32 [16, 128], P('dp'), may hold values from 0 to 31, as said below
- image_target: int32 [16, 128], P('dp'), may hold values from 0 to 31
Outputs:
- attended: bfloat16 [131072, 896], P(('dp', 'bal'))
- grad_latent: float32 [1792, 588], P('bal')
- grad_scale: float32 [1792], P('bal')
Inputs may be any that keep to these rules, and one draw needn't show every extreme that they name: `image_length`: entries of a group come in no fixed order; each length is a multiple of 64; 0 marks an unused entry. The entries bound for one device total at most 256 patches, and those held by one device at most 320; both are reached on some device of every group. Every device of a group sends exactly one image, of at most 128 patches, to one other device and receives exactly one image from one other device; all other entries have image_source equal to image_target. 128 is reached in every group. `quant_scale`: positive.
All inputs are finite; a program needn't handle non-finite values.
Results may differ from a plain program's by a relative error of at most 0.04.
Values may be sent and summed in bfloat16 or wider, within the bound.
A program may use at most 128 MiB of HBM per device.

v0:
```python
import math

import jax
import jax.numpy as jnp
from jax import lax
from jax.sharding import PartitionSpec as P

D = 1792
HEAD = 112
PIX = 588
HEADS = 8
MOVE_ROWS = 128


EPSILON = 1e-06


def quantize(latent, quant_scale):
    ratio = latent.astype(jnp.float32) / quant_scale[:, None]
    level = jnp.floor(ratio + 0.5)
    inside = (level >= -8.0) & (level <= 7.0)
    clipped = jnp.clip(level, -8.0, 7.0)
    quant_weight = (clipped * quant_scale[:, None]).astype(jnp.bfloat16)
    scale_slope = jnp.where(inside, level - ratio, clipped)
    return (quant_weight, inside, scale_slope)


def arrange(length, source, target, member, out_rows, move_rows):
    entries = length.shape[0]
    entry_index = jnp.arange(entries, dtype=jnp.int32)
    before = entry_index[:, None] > entry_index[None, :]
    moving = target != source

    def earlier_total(owner, amounts):
        matching = before & (owner[:, None] == owner[None, :])
        return jnp.sum(jnp.where(matching, amounts[None, :], 0), axis=1)

    target_start = earlier_total(target, length)
    source_start = earlier_total(source, length)
    outbox_start = earlier_total(source, jnp.where(moving, length, 0))
    row_index = jnp.arange(out_rows, dtype=jnp.int32)[:, None]
    covers = (
        (target[None, :] == member)
        & (row_index >= target_start[None, :])
        & (row_index < (target_start + length)[None, :])
    )

    def select_rows(values):
        return jnp.sum(jnp.where(covers, values[None, :], 0), axis=1)

    active = jnp.any(covers, axis=1)
    image_id = select_rows(entry_index)
    within = row_index[:, 0] - select_rows(target_start)
    from_device = select_rows(source)
    from_row = select_rows(source_start) + within
    outbox_row = select_rows(outbox_start) + within
    slot_index = jnp.arange(move_rows, dtype=jnp.int32)[:, None]
    leaving = (
        (source[None, :] == member)
        & moving[None, :]
        & (slot_index >= outbox_start[None, :])
        & (slot_index < (outbox_start + length)[None, :])
    )
    leaving_row = (
        jnp.sum(jnp.where(leaving, (source_start - outbox_start)[None, :], 0), axis=1)
        + slot_index[:, 0]
    )
    leaving_active = jnp.any(leaving, axis=1)
    return (active, image_id, from_device, from_row, outbox_row, leaving_active, leaving_row)


def forward_backward(
    target_pixels,
    active,
    same_image,
    quant_weight,
    embed_bias,
    ln_gain,
    ln_bias,
    project_forward,
    project_backward,
    cot_rows,
    grad_factor,
):
    proj_width = HEADS * HEAD
    score_scale = HEAD ** (-0.5)
    embedded = (
        lax.dot_general(
            target_pixels,
            quant_weight,
            (((1,), (1,)), ((), ())),
            preferred_element_type=jnp.float32,
        )
        + embed_bias
    ).astype(jnp.bfloat16)
    values_row = embedded.astype(jnp.float32)
    row_mean = jnp.mean(values_row, axis=1, keepdims=True)
    centered = values_row - row_mean
    variance = jnp.mean(centered * centered, axis=1, keepdims=True)
    inverse_std = lax.rsqrt(variance + EPSILON)
    centered_scaled = centered * inverse_std
    normed = (centered_scaled * ln_gain + ln_bias).astype(jnp.bfloat16)
    projected = project_forward(normed).astype(jnp.bfloat16)
    row_count = projected.shape[0]
    queries = projected[:, :proj_width].reshape(row_count, HEADS, HEAD)
    key_rows = projected[:, proj_width : 2 * proj_width].reshape(row_count, HEADS, HEAD)
    value_rows = projected[:, 2 * proj_width :].reshape(row_count, HEADS, HEAD)
    scores = (
        jnp.einsum("qhd,khd->hqk", queries, key_rows, preferred_element_type=jnp.float32)
        * score_scale
    )
    exponent = jnp.where(same_image[None], jnp.exp(scores), 0.0)
    denominator = jnp.sum(exponent, axis=2, keepdims=True)
    denominator = jnp.where(active[None, :, None], denominator, 1.0)
    attention = exponent / denominator
    attention_soft = attention.astype(jnp.bfloat16)
    attended = jnp.einsum(
        "hqk,khd->qhd", attention_soft, value_rows, preferred_element_type=jnp.float32
    ).reshape(row_count, proj_width)
    attended = jnp.where(active[:, None], attended, 0.0).astype(jnp.bfloat16)
    grad_out = jnp.where(active[:, None], cot_rows.astype(jnp.float32) * grad_factor, 0.0).astype(
        jnp.bfloat16
    )
    grad_out = grad_out.reshape(row_count, HEADS, HEAD)
    grad_values = jnp.einsum(
        "hqk,qhd->khd", attention_soft, grad_out, preferred_element_type=jnp.float32
    ).astype(jnp.bfloat16)
    grad_attention = jnp.einsum(
        "qhd,khd->hqk", grad_out, value_rows, preferred_element_type=jnp.float32
    )
    row_inner = jnp.sum(attention * grad_attention, axis=2, keepdims=True)
    grad_score = (attention * (grad_attention - row_inner) * score_scale).astype(jnp.bfloat16)
    grad_queries = jnp.einsum(
        "hqk,khd->qhd", grad_score, key_rows, preferred_element_type=jnp.float32
    ).astype(jnp.bfloat16)
    grad_keys = jnp.einsum(
        "hqk,qhd->khd", grad_score, queries, preferred_element_type=jnp.float32
    ).astype(jnp.bfloat16)
    grad_projected = jnp.concatenate(
        [
            grad_queries.reshape(row_count, proj_width),
            grad_keys.reshape(row_count, proj_width),
            grad_values.reshape(row_count, proj_width),
        ],
        axis=1,
    )
    grad_normed = project_backward(grad_projected)
    gained = grad_normed * ln_gain
    grad_rows = inverse_std * (
        gained
        - jnp.mean(gained, axis=1, keepdims=True)
        - centered_scaled * jnp.mean(gained * centered_scaled, axis=1, keepdims=True)
    )
    grad_embedded = jnp.where(active[:, None], grad_rows, 0.0).astype(jnp.bfloat16)
    return (attended, grad_embedded)


def per_device(
    pixels,
    latent,
    quant_scale,
    embed_bias,
    ln_gain,
    ln_bias,
    qkv_weight,
    cotangent,
    image_length,
    image_source,
    image_target,
):
    member = lax.axis_index("bal")
    members = lax.axis_size("bal")
    groups = lax.axis_size("dp")
    out_rows = cotangent.shape[0]
    length = image_length[0]
    source = image_source[0]
    target = image_target[0]
    active, image_id, from_device, from_row, outbox_row, leaving_active, leaving_row = arrange(
        length, source, target, member, out_rows, MOVE_ROWS
    )
    outgoing = jnp.where(
        leaving_active[:, None], jnp.take(pixels, leaving_row, axis=0), jnp.zeros((), pixels.dtype)
    )
    remote = active & (from_device != member)
    local_rows = jnp.where(
        active[:, None], jnp.take(pixels, from_row, axis=0), jnp.zeros((), pixels.dtype)
    )
    wanted_row = from_device * MOVE_ROWS + outbox_row
    arrival_rank = jnp.cumsum(remote.astype(jnp.int32)) - 1
    slot_index = jnp.arange(MOVE_ROWS, dtype=jnp.int32)[:, None]
    matching = remote[None, :] & (arrival_rank[None, :] == slot_index)
    wanted = jnp.where(
        jnp.any(matching, axis=1), jnp.sum(jnp.where(matching, wanted_row[None, :], 0), axis=1), -1
    )
    block_rows = lax.all_gather(outgoing, "bal", axis=0, tiled=True)
    columns = jnp.arange(block_rows.shape[0], dtype=jnp.int32)
    selector = (wanted[:, None] == columns[None, :]).astype(jnp.bfloat16)
    incoming = jnp.dot(selector, block_rows, preferred_element_type=jnp.float32).astype(
        jnp.bfloat16
    )
    arrived_rows = jnp.take(incoming, jnp.clip(arrival_rank, 0, MOVE_ROWS - 1), axis=0)
    target_pixels = jnp.where(remote[:, None], arrived_rows, local_rows)
    same_image = (image_id[:, None] == image_id[None, :]) & active[:, None] & active[None, :]
    quant_weight, inside, scale_slope = quantize(latent, quant_scale)
    grad_factor = 1.0 / math.sqrt(groups * members * out_rows)
    lsq_factor = 1.0 / math.sqrt(PIX * 7.0)
    whole_weight = lax.all_gather(qkv_weight, "dp", axis=1, tiled=True)

    def project_forward(normed):
        return jnp.dot(normed, whole_weight, preferred_element_type=jnp.float32)

    def project_backward(grad_projected):
        return lax.dot_general(
            grad_projected,
            whole_weight,
            (((1,), (1,)), ((), ())),
            preferred_element_type=jnp.float32,
        )

    attended, grad_embedded = forward_backward(
        target_pixels,
        active,
        same_image,
        quant_weight,
        embed_bias,
        ln_gain,
        ln_bias,
        project_forward,
        project_backward,
        cotangent,
        grad_factor,
    )
    row_share = D // members
    device_grad = lax.dot_general(
        grad_embedded, target_pixels, (((0,), (0,)), ((), ())), preferred_element_type=jnp.float32
    )
    rounded = lax.optimization_barrier(device_grad.astype(jnp.bfloat16)).astype(jnp.float32)
    scale_total = lax.psum(jnp.sum(rounded * scale_slope, axis=1), ("dp", "bal"))
    group_rows = lax.psum_scatter(
        rounded.astype(jnp.bfloat16), "bal", scatter_dimension=0, tiled=True
    )
    summed = lax.psum(group_rows, "dp").astype(jnp.float32)
    row_start = member * row_share
    inside_rows = lax.dynamic_slice_in_dim(inside, row_start, row_share, 0)
    grad_latent = jnp.where(inside_rows, summed, 0.0)
    grad_scale = lsq_factor * lax.dynamic_slice_in_dim(scale_total, row_start, row_share, 0)
    return (attended, grad_latent, grad_scale)


def solution(mesh):
    placed = (
        P(("dp", "bal"), None),
        P(),
        P(),
        P(),
        P(),
        P(),
        P(None, "dp"),
        P(("dp", "bal"), None),
        P("dp", None),
        P("dp", None),
        P("dp", None),
    )
    return jax.shard_map(
        per_device,
        mesh=mesh,
        in_specs=placed,
        out_specs=(P(("dp", "bal"), None), P("bal", None), P("bal")),
        check_vma=False,
    )
```

profile of v0, /device:TPU:1, one launch (start us, length us, event | category | flops | bytes accessed | tf_op | source)
XLA Modules:
  0.0 511.6 jit_solution(3995761419418180671)
XLA Ops:
  8.7 0.9 select_reduce_fusion.8
  10.5 0.9 gather_fusion
  13.8 1.9 gather_fusion.2
  16.8 64.1 %all-gather.3.cloned.1.call-done = bf16[4096,588]{1,0:T(8,128)(2,1)} async-done(((bf16[128,588]{1,0:T(8,128)(2,1)}), bf16[4096,588]{1,0:T(8,128)(2,1)}) %all-gather.3.cloned.1.call-update) | async-done | bytes 4816912 | tf_op jit(solution)/shard_map/all_gather | solution.py:195
  80.9 4.6 fusion.34
  85.7 1.9 gather_fusion.1
  87.7 2.6 fusion.86
  90.2 1.3 copy-done.3
  91.9 108.6 %all-gather.5.cloned.1.call-done = bf16[1792,2688]{0,1:T(8,128)(2,1)} async-done(((bf16[1792,168]{0,1:T(8,128)(2,1)}), bf16[1792,2688]{0,1:T(8,128)(2,1)}) %all-gather.5.cloned.1.call-update) | async-done | bytes 9633808 | tf_op jit(solution)/shard_map/all_gather | solution.py:207
  200.5 7.2 %convolution_convert_fusion = bf16[256,2688]{1,0:T(8,128)(2,1)S(1)} fusion(bf16[1792,2688]{0,1:T(8,128)(2,1)} %all-gather.5.cloned.1.call-done, f32[256,1792]{1,0:T(8,128)} %copy-done.3, f32[1792]{0:T(1024)S(1)} %copy-done.13, f32[1792]{0:T(1024)S(1)} %copy-done.14, f32[256]{0:T(256)S(1)} %add_rsqrt_fusion, f32[256]{0:T(256)S(1)} %broadcast_multiply_fusion.2), kind=kOutput, calls=%fused_computation.12 | convolution fusion | flops 2469232640 | bytes 12861440 | tf_op jit(solution)/shard_map/dot_general | solution.py:210
  208.3 1.9 fusion.22
  211.0 4.5 fusion.28
  215.5 4.7 fusion.31
  220.2 2.4 convolution_convert_fusion.2
  222.6 7.0 %fusion.82 = (f32[256]{0:T(256)S(1)}, f32[256]{0:T(256)S(1)}, f32[256,1792]{1,0:T(8,128)S(1)}) fusion(f32[256]{0:T(256)S(1)} %add_rsqrt_fusion, f32[256,1792]{1,0:T(8,128)S(1)} %copy-done.4, f32[256]{0:T(256)S(1)} %broadcast_multiply_fusion.2, f32[1792]{0:T(1024)S(1)} %copy-done.14, bf16[1792,2688]{0,1:T(8,128)(2,1)} %all-gather.5.cloned.1.call-done, ...), kind=kOutput, calls=%fused_computation.141 | convolution fusion | flops 2473131520 | bytes 14691328 | tf_op jit(solution)/shard_map/dot_general | solution.py:213
  229.7 1.2 convolution_convert_fusion.1
  230.9 4.9 multiply_reduce_fusion
  236.6 1.3 dynamic-slice
  239.3 1.0 copy.60
  240.3 103.2 %psum.15 = f32[1792]{0:T(1024)S(1)} all-reduce(f32[1792]{0:T(1024)S(1)} %get-tuple-element.25), channel_id=1, replica_groups=mesh['dp'=16,'bal'=32] {'dp','bal'}, use_global_device_ids=true, to_apply=%region_24.25 | all-reduce | flops 1792 | bytes 14336 | tf_op jit(solution)/shard_map/psum | solution.py:238
  343.5 32.6 %all-reduce.6.cloned.1.call-done = bf16[1792,588]{0,1:T(8,128)(2,1)} async-done(((bf16[1792,588]{0,1:T(8,128)(2,1)}), bf16[1792,588]{0,1:T(8,128)(2,1)}) %all-reduce.6.cloned.1.call-update) | async-done | bytes 2107408
  376.1 1.8 constant_dynamic-slice_fusion
  378.5 124.6 %all-reduce.4.cloned.1.call-done = bf16[56,588]{0,1:T(8,128)(2,1)} async-done(((bf16[56,588]{0,1:T(8,128)(2,1)}), bf16[56,588]{0,1:T(8,128)(2,1)}) %all-reduce.4.cloned.1.call-update) | async-done | bytes 65872 | tf_op jit(solution)/shard_map/psum | solution.py:242
  503.1 1.1 convert_select_fusion
  (89 shorter events, 10.5 us)
Async XLA Ops:
  7.2 3.4 copy-start
  7.2 5.9 %copy-start.10 = (s32[1,128]{1,0:T(1,128)S(1)}, s32[1,128]{1,0:T(1,128)}, u32[]{:S(2)}) copy-start(s32[1,128]{1,0:T(1,128)} %param.20) | copy-start | bytes 1540
  7.2 73.7 %all-gather.3.cloned.1.call-start = ((), (), s32[]{:S(2)}) async-start(), calls=%async_computation | async-start | bytes 5406720 | tf_op jit(solution)/shard_map/all_gather | solution.py:195
  11.4 4.4 copy-start.5
  12.2 188.3 %all-gather.5.cloned.1.call-start = ((), (), s32[]{:S(2)}) async-start(), calls=%async_computation.1 | async-start | bytes 10235904 | tf_op jit(solution)/shard_map/all_gather | solution.py:207
  85.5 2.1 copy-start.2
  85.5 2.1 copy-start.11
  85.5 2.1 copy-start.12
  87.6 112.9 %copy-start.13 = (f32[1792]{0:T(1024)S(1)}, f32[1792]{0:T(1024)}, u32[]{:S(2)}) copy-start(f32[1792]{0:T(1024)} %param.16) | copy-start | bytes 21508
  87.6 112.9 %copy-start.14 = (f32[1792]{0:T(1024)S(1)}, f32[1792]{0:T(1024)}, u32[]{:S(2)}) copy-start(f32[1792]{0:T(1024)} %param.15) | copy-start | bytes 21508
  90.2 1.3 copy-start.3
  208.1 2.4 copy-start.6
  208.3 2.2 copy-start.7
  220.2 2.4 copy-start.4
  220.2 2.4 copy-start.15
  220.2 2.4 copy-start.16
  222.6 7.1 %copy-start.8 = (bf16[256,588]{1,0:T(8,128)(2,1)S(1)}, bf16[256,588]{1,0:T(8,128)(2,1)}, u32[]{:S(2)}) copy-start(bf16[256,588]{1,0:T(8,128)(2,1)} %gather_fusion.2) | copy-start | bytes 903172
  222.6 7.1 %copy-start.9 = (bf16[256,588]{1,0:T(8,128)(2,1)S(1)}, bf16[256,588]{1,0:T(8,128)(2,1)}, u32[]{:S(2)}) copy-start(bf16[256,588]{1,0:T(8,128)(2,1)} %gather_fusion.1) | copy-start | bytes 903172
  230.9 5.0 copy-start.1
  235.9 140.2 %all-reduce.6.cloned.1.call-start = ((), (), s32[]{:S(2)}) async-start(), calls=%async_computation.3 | async-start | bytes 4243456
  235.9 2.7 copy-start.17
  236.6 266.5 %all-reduce.4.cloned.1.call-start = ((), (), s32[]{:S(2)}) async-start(), calls=%async_computation.2 | async-start | bytes 303104 | tf_op jit(solution)/shard_map/psum | solution.py:242
Sparse Core Ops, SparseCore 0:
  12.4 68.4 all-gather.2
  83.0 117.4 all-gather.4
  240.0 136.0 all-reduce.5
  378.4 124.6 all-reduce.3
where the time goes:
time: 521 us; the launch traced here: 512 us
  waiting for transfers between devices  331 us (64%)
  blocking collectives  103 us (20%)
  matrix products  37.3 us (7%)
  between operations  14.8 us (3%)
  other arithmetic  12.6 us (2%)
  local copies, waits for them, and re-layouts  12.2 us (2%)
    psum x1, waiting for transfers between devices, per_device(): summed = lax.psum(group_rows, 'dp').astype(jnp.float32)  125 us
    all_gather x1, waiting for transfers between devices, per_device(): whole_weight = lax.all_gather(qkv_weight, 'dp', axis=1, tiled=True)  109 us
    psum x1, blocking collectives, per_device(): lax.psum(jnp.sum(rounded * scale_slope, axis=1), ('dp', 'bal'))  103 us
    all_gather x1, waiting for transfers between devices, per_device(): block_rows = lax.all_gather(outgoing, 'bal', axis=0, tiled=True)  64.1 us
    unnamed x5, waiting for transfers between devices  34 us
  transfers between devices with their start and end apart: 4, of which 4 were waited for; matrix products, arithmetic and copies ran while one was open for 3% of the time, Pallas kernels for 0%

commit v1 on v0

--- a/solution.py
+++ b/solution.py
@@ -1,8 +1,11 @@
+import functools
 import math
 
 import jax
 import jax.numpy as jnp
 from jax import lax
+from jax.experimental import pallas as pl
+from jax.experimental.pallas import tpu as pltpu
 from jax.sharding import PartitionSpec as P
 
 D = 1792
@@ -153,6 +156,603 @@
     )
     grad_embedded = jnp.where(active[:, None], grad_rows, 0.0).astype(jnp.bfloat16)
     return (attended, grad_embedded)
+
+
+MESH = pl.DeviceIdType.MESH
+SHARD = 168
+CHIP_ROWS = 112
+HALF_COLS = 8 * SHARD
+PIX_PAD = 640
+PIECES = 20
+GROUP_ROWS = ((0, 64, 32), (64, 48, 32))
+
+
+def place():
+    z = lax.axis_index("dp")
+    b = lax.axis_index("bal")
+    core = lax.rem(b, 2)
+    x = lax.rem(b // 2, 4)
+    y = b // 8
+    return z, b, x, y, core
+
+
+def remote(src, dst, send, recv, device):
+    copy = pltpu.make_async_remote_copy(
+        src_ref=src, dst_ref=dst, send_sem=send, recv_sem=recv, device_id=device, device_id_type=MESH
+    )
+    return copy
+
+
+def gather_kernel(
+    w_ref,
+    pieces_ref,
+    source_ref,
+    weight_ref,
+    arrived_ref,
+    ring,
+    inbox,
+    stage,
+    ring_send,
+    ring_recv,
+    out_send,
+    out_recv,
+    back_send,
+    back_recv,
+    plane_send,
+    plane_recv,
+    pair_send,
+    pair_recv,
+):
+    z, b, x, y, core = place()
+    up = lax.rem(z + 1, 16)
+    down = lax.rem(z + 15, 16)
+    direction = 1 - 2 * core
+    ring_to = lax.rem(z + direction + 16, 16)
+    sibling = b + 1 - 2 * core
+    chip = b // 2
+
+    barrier = pltpu.get_barrier_semaphore()
+
+    def greet(step, carry):
+        pl.semaphore_signal(
+            barrier, inc=1, device_id=(z, lax.rem(b + step, 32)), device_id_type=MESH
+        )
+        return carry
+
+    lax.fori_loop(1, 32, greet, 0)
+    for other in (up, down):
+        pl.semaphore_signal(barrier, inc=1, device_id=(other, b), device_id_type=MESH)
+    pl.semaphore_wait(barrier, 33)
+
+    chip_rows = pl.ds(pl.multiple_of(chip * CHIP_ROWS, 16), CHIP_ROWS)
+    ring[0] = w_ref[chip_rows, :]
+
+    def ring_copy(step):
+        return remote(
+            ring.at[step],
+            ring.at[step + 1],
+            ring_send.at[step],
+            ring_recv.at[step + 1],
+            (ring_to, b),
+        )
+
+    def out_copy(target, slot):
+        return remote(
+            pieces_ref.at[target], inbox.at[slot], out_send.at[target], out_recv.at[slot], (z, target)
+        )
+
+    def back_copy(target, slot):
+        return remote(
+            stage.at[target],
+            arrived_ref.at[slot],
+            back_send.at[target],
+            back_recv.at[slot],
+            (z, target),
+        )
+
+    ring_copy(0).start()
+
+    def send_out(step, carry):
+        target = lax.rem(b + step, 32)
+
+        @pl.when(target < PIECES)
+        def _():
+            out_copy(target, b).start()
+
+        return carry
+
+    lax.fori_loop(1, 32, send_out, 0)
+    ring_copy(0).wait_recv()
+    ring_copy(1).start()
+
+    @pl.when(b < PIECES)
+    def _():
+        inbox[b] = pieces_ref[b]
+
+        def take(step, carry):
+            out_copy(b, lax.rem(b + step, 32)).wait_recv()
+            return carry
+
+        lax.fori_loop(1, 32, take, 0)
+
+    ring_copy(1).wait_recv()
+    ring_copy(2).start()
+
+    @pl.when(b < PIECES)
+    def _():
+        arrived_ref[b] = inbox[source_ref[b]]
+
+        def send_back(step, carry):
+            target = lax.rem(b + step, 32)
+            stage[target] = inbox[source_ref[target]]
+            back_copy(target, b).start()
+            return carry
+
+        lax.fori_loop(1, 32, send_back, 0)
+
+    for step in range(3, 7):
+        ring_copy(step - 1).wait_recv()
+        ring_copy(step).start()
+    ring_copy(6).wait_recv()
+
+    @pl.when(core == 0)
+    def _():
+        ring_copy(7).start()
+        ring_copy(7).wait_recv()
+
+    parts = []
+    for j in range(8):
+        below = lax.rem(z - j - 1 + 16, 8) + 1
+        above = lax.rem(j - z + 16, 8)
+        parts.append(ring[below * (1 - core) + above * core])
+    weight_ref[core, chip_rows, :] = jnp.concatenate(parts, axis=1)
+
+    def chip_at(group, first, second):
+        swap = lax.rem(core + group, 2)
+        dx = first * (1 - swap) + second * swap
+        dy = first * swap + second * (1 - swap)
+        return lax.rem(y + dy + 4, 4) * 4 + lax.rem(x + dx + 4, 4)
+
+    def block(group, where, low=0, count=None):
+        start, rows, _ = GROUP_ROWS[group]
+        if count is None:
+            count = rows - low
+        first = pl.multiple_of(where * CHIP_ROWS + start + low, 16)
+        return weight_ref.at[core, pl.ds(first, count), :]
+
+    def plane_copy(group, index, sent, to, low=0, count=None):
+        rows = block(group, sent, low, count)
+        return remote(
+            rows,
+            rows,
+            plane_send.at[group, index],
+            plane_recv.at[group, index],
+            (z, to * 2 + core),
+        )
+
+    offsets = (0, -1, 1, 2)
+
+    def first_copy(group, kind, origin=0):
+        lower = GROUP_ROWS[group][2]
+        to = chip_at(group, 1 if kind in (0, 2) else -1, 0)
+        sent = chip_at(group, (0, 0, -1, 1)[kind] + origin, 0)
+        low, count = ((0, None), (0, None), (0, lower), (lower, None))[kind]
+        return plane_copy(group, kind, sent, to, low, count)
+
+    def first_wait(group, kind):
+        lower = GROUP_ROWS[group][2]
+        low, count = ((0, None), (0, None), (0, lower), (lower, None))[kind]
+        sent = chip_at(group, (-1, 1, 2, 2)[kind], 0)
+        plane_copy(group, kind, sent, 0, low, count).wait_recv()
+
+    def second_copy(group, place_index, kind):
+        lower = GROUP_ROWS[group][2]
+        a = offsets[place_index]
+        to = chip_at(group, 0, 1 if kind in (0, 2) else -1)
+        sent = chip_at(group, a, (0, 0, -1, 1)[kind])
+        low, count = ((0, None), (0, None), (0, lower), (lower, None))[kind]
+        return plane_copy(group, 4 + 4 * place_index + kind, sent, to, low, count)
+
+    def second_wait(group, place_index, kind):
+        lower = GROUP_ROWS[group][2]
+        a = offsets[place_index]
+        low, count = ((0, None), (0, None), (0, lower), (lower, None))[kind]
+        sent = chip_at(group, a, (-1, 1, 2, 2)[kind])
+        plane_copy(group, 4 + 4 * place_index + kind, sent, 0, low, count).wait_recv()
+
+    def pair_copy(group, place_index, second_index):
+        rows = block(group, chip_at(group, offsets[place_index], offsets[second_index]))
+        index = place_index * 4 + second_index
+        return remote(
+            rows, rows, pair_send.at[group, index], pair_recv.at[group, index], (z, sibling)
+        )
+
+    groups = (0, 1)
+    for g in groups:
+        first_copy(g, 0).start()
+        first_copy(g, 1).start()
+    for g in groups:
+        second_copy(g, 0, 0).start()
+        second_copy(g, 0, 1).start()
+        pair_copy(g, 0, 0).start()
+    for kind, index in ((0, 1), (1, 2)):
+        for g in groups:
+            first_wait(g, kind)
+            first_copy(g, kind + 2).start()
+            second_copy(g, index, 0).start()
+            second_copy(g, index, 1).start()
+            pair_copy(g, index, 0).start()
+    for g in groups:
+        first_wait(g, 2)
+        first_wait(g, 3)
+        second_copy(g, 3, 0).start()
+        second_copy(g, 3, 1).start()
+        pair_copy(g, 3, 0).start()
+    for index in range(4):
+        for kind in (0, 1):
+            for g in groups:
+                second_wait(g, index, kind)
+                second_copy(g, index, kind + 2).start()
+                pair_copy(g, index, kind + 1).start()
+    for index in range(4):
+        for g in groups:
+            second_wait(g, index, 2)
+            second_wait(g, index, 3)
+            pair_copy(g, index, 3).start()
+
+    for step in range(7):
+        ring_copy(step).wait_send()
+
+    @pl.when(core == 0)
+    def _():
+        ring_copy(7).wait_send()
+
+    def sent_out(step, carry):
+        target = lax.rem(b + step, 32)
+
+        @pl.when(target < PIECES)
+        def _():
+            out_copy(target, b).wait_send()
+
+        return carry
+
+    lax.fori_loop(1, 32, sent_out, 0)
+
+    @pl.when(b < PIECES)
+    def _():
+        def sent_back(step, carry):
+            back_copy(lax.rem(b + step, 32), b).wait_send()
+            return carry
+
+        lax.fori_loop(1, 32, sent_back, 0)
+
+    def arrive(step, carry):
+        slot = lax.rem(b + step, 32)
+
+        @pl.when(slot < PIECES)
+        def _():
+            back_copy(b, slot).wait_recv()
+
+        return carry
+
+    lax.fori_loop(1, 32, arrive, 0)
+    for g in groups:
+        for kind in range(4):
+            first_copy(g, kind).wait_send()
+            for index in range(4):
+                second_copy(g, index, kind).wait_send()
+        for index in range(4):
+            for second in range(4):
+                pair_copy(g, index, second).wait_send()
+                start, rows, _ = GROUP_ROWS[g]
+                swap = 1 - lax.rem(core + g, 2)
+                dx = offsets[index] * (1 - swap) + offsets[second] * swap
+                dy = offsets[index] * swap + offsets[second] * (1 - swap)
+                where = lax.rem(y + dy + 4, 4) * 4 + lax.rem(x + dx + 4, 4)
+                first = pl.multiple_of(where * CHIP_ROWS + start, 16)
+                rows_ref = weight_ref.at[1 - core, pl.ds(first, rows), :]
+                remote(
+                    rows_ref,
+                    rows_ref,
+                    pair_send.at[g, index * 4 + second],
+                    pair_recv.at[g, index * 4 + second],
+                    (z, sibling),
+                ).wait_recv()
+
+
+def gather_weight(weight, pieces, source):
+    vmem = pl.BlockSpec(memory_space=pltpu.VMEM)
+    dma = pltpu.SemaphoreType.DMA
+    return pl.pallas_call(
+        gather_kernel,
+        name="gather_weight",
+        out_shape=(
+            jax.ShapeDtypeStruct((2, D, HALF_COLS), jnp.bfloat16),
+            jax.ShapeDtypeStruct((PIECES, 32, 128), jnp.bfloat16),
+        ),
+        in_specs=[vmem, vmem, pl.BlockSpec(memory_space=pltpu.SMEM)],
+        out_specs=(vmem, vmem),
+        scratch_shapes=[
+            pltpu.VMEM((9, CHIP_ROWS, SHARD), jnp.bfloat16),
+            pltpu.VMEM((32, 32, 128), jnp.bfloat16),
+            pltpu.VMEM((32, 32, 128), jnp.bfloat16),
+            dma((9,)),
+            dma((9,)),
+            dma((32,)),
+            dma((32,)),
+            dma((32,)),
+            dma((32,)),
+            dma((2, 20)),
+            dma((2, 20)),
+            dma((2, 16)),
+            dma((2, 16)),
+        ],
+        compiler_params=pltpu.CompilerParams(
+            collective_id=0, has_side_effects=True, vmem_limit_bytes=40 * 1024 * 1024
+        ),
+    )(weight, pieces, source)
+
+
+def reduce_kernel(
+    grad_ref,
+    out_ref,
+    twin,
+    held,
+    across,
+    line,
+    met,
+    tiles,
+    total,
+    result,
+    twin_send,
+    twin_recv,
+    across_send,
+    across_recv,
+    line_send,
+    line_recv,
+    tile_send,
+    tile_recv,
+    total_send,
+    total_recv,
+    last_send,
+    last_recv,
+):
+    z, b, x, y, core = place()
+    sibling = b + 1 - 2 * core
+    first = x * (1 - core) + y * core
+    second = y * (1 - core) + x * core
+
+    def chip_of(which, f, s):
+        return (s * 4 + f) * (1 - which) + (f * 4 + s) * which
+
+    def target_chip(which, a, half):
+        mine = x * (1 - which) + y * which
+        f = lax.rem(mine + a, 4)
+        return chip_of(which, f, 2 * half + lax.rem(f + which, 2))
+
+    def at(f, s):
+        return (z, chip_of(core, f, s) * 2 + core)
+
+    barrier = pltpu.get_barrier_semaphore()
+    pl.semaphore_signal(barrier, inc=1, device_id=(z, sibling), device_id_type=MESH)
+    for a in range(1, 4):
+        pl.semaphore_signal(
+            barrier, inc=1, device_id=at(lax.rem(first + a, 4), second), device_id_type=MESH
+        )
+        pl.semaphore_signal(
+            barrier, inc=1, device_id=at(first, lax.rem(second + a, 4)), device_id_type=MESH
+        )
+
+    def greet(step, carry):
+        pl.semaphore_signal(
+            barrier, inc=1, device_id=(lax.rem(z + step, 16), b), device_id_type=MESH
+        )
+        return carry
+
+    lax.fori_loop(1, 16, greet, 0)
+    pl.semaphore_wait(barrier, 22)
+
+    def twin_copy(a, half):
+        chip = target_chip(1 - core, a, half)
+        return remote(
+            grad_ref.at[chip], twin.at[a, half], twin_send.at[a, half], twin_recv.at[a, half], (z, sibling)
+        )
+
+    order = (2, 1, 3, 0)
+    for a in order:
+        for half in range(2):
+            twin_copy(a, half).start()
+
+    def across_copy(a):
+        return remote(
+            held.at[a],
+            across.at[a],
+            across_send.at[a],
+            across_recv.at[a],
+            at(lax.rem(first + a, 4), second),
+        )
+
+    for a in order:
+        for half in range(2):
+            twin_copy(a, half).wait_recv()
+            chip = target_chip(core, a, half)
+            held[a, half] = (
+                grad_ref[chip].astype(jnp.float32) + twin[a, half].astype(jnp.float32)
+            ).astype(jnp.bfloat16)
+        if a > 0:
+            across_copy(a).start()
+    for a in (1, 3, 2):
+        across_copy(a).wait_recv()
+    for half in range(2):
+        line[half] = (
+            held[0, half].astype(jnp.float32)
+            + across[1, half].astype(jnp.float32)
+            + across[2, half].astype(jnp.float32)
+            + across[3, half].astype(jnp.float32)
+        ).astype(jnp.bfloat16)
+
+    parity = lax.rem(first + core, 2)
+    owner = lax.rem(first + second, 2) == core
+
+    def line_copy(half):
+        to = 2 * half + parity
+        away = lax.rem(to - second + 4, 4)
+        return remote(
+            line.at[half],
+            met.at[away],
+            line_send.at[half],
+            line_recv.at[away],
+            at(first, to),
+        )
+
+    for a in range(1, 4):
+        across_copy(a).wait_send()
+    for half in range(2):
+        to = 2 * half + parity
+
+        @pl.when(to != second)
+        def _():
+            line_copy(half).start()
+
+    tile = total.shape[1]
+
+    def tile_copy(index):
+        to = 2 * index
+        return remote(
+            result.at[pl.ds(16 * index, 16)],
+            tiles.at[z],
+            tile_send.at[index],
+            tile_recv.at[z],
+            (to, b),
+        )
+
+    def tile_wait(slot):
+        remote(
+            result.at[pl.ds(0, 16)], tiles.at[slot], tile_send.at[0], tile_recv.at[slot], (slot, b)
+        ).wait_recv()
+
+    def total_copy(to, index):
+        return remote(
+            total.at[index],
+            total.at[index],
+            total_send.at[to],
+            total_recv.at[index],
+            (to, b),
+        )
+
+    @pl.when(owner)
+    def _():
+        mine = line[second // 2].astype(jnp.float32)
+        for away in (1, 3, 2):
+            remote(
+                line.at[0], met.at[away], line_send.at[0], line_recv.at[away], (z, sibling)
+            ).wait_recv()
+            mine = mine + met[away].astype(jnp.float32)
+        result[...] = mine.astype(jnp.bfloat16)
+        for index in range(7):
+
+            @pl.when(z != 2 * index)
+            def _():
+                tile_copy(index).start()
+
+        @pl.when((z < 14) & (lax.rem(z, 2) == 0))
+        def _():
+            index = z // 2
+            tiles[z] = result[pl.ds(pl.multiple_of(16 * index, 16), 16), :]
+
+            def take(step, carry):
+                tile_wait(lax.rem(z + step, 16))
+                return carry
+
+            lax.fori_loop(1, 16, take, 0)
+            value = tiles[0].astype(jnp.float32)
+            for slot in range(1, 16):
+                value = value + tiles[slot].astype(jnp.float32)
+            total[index] = value.astype(jnp.bfloat16)
+
+            def spread(step, carry):
+                total_copy(lax.rem(z + step, 16), index).start()
+                return carry
+
+            lax.fori_loop(1, 16, spread, 0)
+
+        for index in range(7):
+
+            @pl.when(z != 2 * index)
+            def _():
+                total_copy(0, index).wait_recv()
+
+        remote(total, total, last_send, last_recv, (z, sibling)).start()
+
+        for index in range(7):
+
+            @pl.when(z != 2 * index)
+            def _():
+                tile_copy(index).wait_send()
+
+        @pl.when((z < 14) & (lax.rem(z, 2) == 0))
+        def _():
+            def spent(step, carry):
+                total_copy(lax.rem(z + step, 16), z // 2).wait_send()
+                return carry
+
+            lax.fori_loop(1, 16, spent, 0)
+
+        remote(total, total, last_send, last_recv, (z, sibling)).wait_send()
+
+    @pl.when(jnp.logical_not(owner))
+    def _():
+        remote(total, total, last_send, last_recv, (z, sibling)).wait_recv()
+
+    for a in range(4):
+        for half in range(2):
+            twin_copy(a, half).wait_send()
+    for half in range(2):
+        to = 2 * half + parity
+
+        @pl.when(to != second)
+        def _():
+            line_copy(half).wait_send()
+
+    out_ref[...] = total[...]
+
+
+def reduce_grad(grad):
+    vmem = pl.BlockSpec(memory_space=pltpu.VMEM)
+    dma = pltpu.SemaphoreType.DMA
+    block = (CHIP_ROWS, PIX_PAD)
+    return pl.pallas_call(
+        reduce_kernel,
+        name="reduce_grad",
+        out_shape=jax.ShapeDtypeStruct((7, 16, PIX_PAD), jnp.bfloat16),
+        in_specs=[vmem],
+        out_specs=vmem,
+        scratch_shapes=[
+            pltpu.VMEM((4, 2) + block, jnp.bfloat16),
+            pltpu.VMEM((4, 2) + block, jnp.bfloat16),
+            pltpu.VMEM((4, 2) + block, jnp.bfloat16),
+            pltpu.VMEM((2,) + block, jnp.bfloat16),
+            pltpu.VMEM((4,) + block, jnp.bfloat16),
+            pltpu.VMEM((16, 16, PIX_PAD), jnp.bfloat16),
+            pltpu.VMEM((7, 16, PIX_PAD), jnp.bfloat16),
+            pltpu.VMEM(block, jnp.bfloat16),
+            dma((4, 2)),
+            dma((4, 2)),
+            dma((4,)),
+            dma((4,)),
+            dma((2,)),
+            dma((4,)),
+            dma((7,)),
+            dma((16,)),
+            dma((16,)),
+            dma((7,)),
+            dma,
+            dma,
+        ],
+        compiler_params=pltpu.CompilerParams(
+            collective_id=1, has_side_effects=True, vmem_limit_bytes=40 * 1024 * 1024
+        ),
+    )(grad)
 
 
 def per_device(
@@ -178,47 +778,52 @@
     active, image_id, from_device, from_row, outbox_row, leaving_active, leaving_row = arrange(
         length, source, target, member, out_rows, MOVE_ROWS
     )
-    outgoing = jnp.where(
-        leaving_active[:, None], jnp.take(pixels, leaving_row, axis=0), jnp.zeros((), pixels.dtype)
-    )
-    remote = active & (from_device != member)
-    local_rows = jnp.where(
-        active[:, None], jnp.take(pixels, from_row, axis=0), jnp.zeros((), pixels.dtype)
-    )
-    wanted_row = from_device * MOVE_ROWS + outbox_row
-    arrival_rank = jnp.cumsum(remote.astype(jnp.int32)) - 1
-    slot_index = jnp.arange(MOVE_ROWS, dtype=jnp.int32)[:, None]
-    matching = remote[None, :] & (arrival_rank[None, :] == slot_index)
-    wanted = jnp.where(
-        jnp.any(matching, axis=1), jnp.sum(jnp.where(matching, wanted_row[None, :], 0), axis=1), -1
-    )
-    block_rows = lax.all_gather(outgoing, "bal", axis=0, tiled=True)
-    columns = jnp.arange(block_rows.shape[0], dtype=jnp.int32)
-    selector = (wanted[:, None] == columns[None, :]).astype(jnp.bfloat16)
-    incoming = jnp.dot(selector, block_rows, preferred_element_type=jnp.float32).astype(
-        jnp.bfloat16
-    )
-    arrived_rows = jnp.take(incoming, jnp.clip(arrival_rank, 0, MOVE_ROWS - 1), axis=0)
-    target_pixels = jnp.where(remote[:, None], arrived_rows, local_rows)
+    padded = jnp.pad(pixels, ((0, 0), (0, PIX_PAD - PIX)))
+    rows_in = jnp.arange(pixels.shape[0], dtype=jnp.int32)[None, :]
+    leaving = leaving_active[:, None] & (leaving_row[:, None] == rows_in)
+    outgoing = jnp.dot(
+        leaving.astype(jnp.bfloat16), padded, preferred_element_type=jnp.float32
+    ).astype(jnp.bfloat16)
+    pieces = outgoing.reshape(4, 32, 5, 128).transpose(0, 2, 1, 3).reshape(PIECES, 32, 128)
+    moving = (target != source) & (length > 0)
+    receivers = jnp.arange(members, dtype=jnp.int32)[:, None]
+    sender = jnp.sum(
+        jnp.where((target[None, :] == receivers) & moving[None, :], source[None, :], 0), axis=1
+    )
+    weight, arrived = gather_weight(qkv_weight, pieces, sender)
+    arrived_rows = arrived.reshape(4, 5, 32, 128).transpose(0, 2, 1, 3).reshape(MOVE_ROWS, PIX_PAD)
+    remote_row = from_device != member
+    wanted = jnp.where(remote_row, pixels.shape[0] + outbox_row, from_row)
+    columns = jnp.arange(pixels.shape[0] + MOVE_ROWS, dtype=jnp.int32)[None, :]
+    selector = (active[:, None] & (wanted[:, None] == columns)).astype(jnp.bfloat16)
+    target_pixels = jnp.dot(
+        selector, jnp.concatenate([padded, arrived_rows], axis=0), preferred_element_type=jnp.float32
+    ).astype(jnp.bfloat16)
     same_image = (image_id[:, None] == image_id[None, :]) & active[:, None] & active[None, :]
     quant_weight, inside, scale_slope = quantize(latent, quant_scale)
     grad_factor = 1.0 / math.sqrt(groups * members * out_rows)
     lsq_factor = 1.0 / math.sqrt(PIX * 7.0)
-    whole_weight = lax.all_gather(qkv_weight, "dp", axis=1, tiled=True)
+    slot = jnp.arange(HALF_COLS, dtype=jnp.int32)[None, :] // SHARD
+    plane = lax.axis_index("dp")
+    low_first = lax.rem(plane - slot + 15, 16) < 8
 
     def project_forward(normed):
-        return jnp.dot(normed, whole_weight, preferred_element_type=jnp.float32)
+        zero = jnp.dot(normed, weight[0], preferred_element_type=jnp.float32)
+        one = jnp.dot(normed, weight[1], preferred_element_type=jnp.float32)
+        return jnp.concatenate(
+            [jnp.where(low_first, zero, one), jnp.where(low_first, one, zero)], axis=1
+        )
 
     def project_backward(grad_projected):
+        low, high = grad_projected[:, :HALF_COLS], grad_projected[:, HALF_COLS:]
+        zero, one = jnp.where(low_first, low, high), jnp.where(low_first, high, low)
+        contract = (((1,), (1,)), ((), ()))
         return lax.dot_general(
-            grad_projected,
-            whole_weight,
-            (((1,), (1,)), ((), ())),
-            preferred_element_type=jnp.float32,
-        )
+            zero, weight[0], contract, preferred_element_type=jnp.float32
+        ) + lax.dot_general(one, weight[1], contract, preferred_element_type=jnp.float32)
 
     attended, grad_embedded = forward_backward(
-        target_pixels,
+        target_pixels[:, :PIX],
         active,
         same_image,
         quant_weight,
@@ -234,16 +839,15 @@
     device_grad = lax.dot_general(
         grad_embedded, target_pixels, (((0,), (0,)), ((), ())), preferred_element_type=jnp.float32
     )
-    rounded = lax.optimization_barrier(device_grad.astype(jnp.bfloat16)).astype(jnp.float32)
-    scale_total = lax.psum(jnp.sum(rounded * scale_slope, axis=1), ("dp", "bal"))
-    group_rows = lax.psum_scatter(
-        rounded.astype(jnp.bfloat16), "bal", scatter_dimension=0, tiled=True
-    )
-    summed = lax.psum(group_rows, "dp").astype(jnp.float32)
+    blocks = device_grad.astype(jnp.bfloat16).reshape(D // CHIP_ROWS, CHIP_ROWS, PIX_PAD)
+    reduced = reduce_grad(blocks).reshape(CHIP_ROWS, PIX_PAD)
+    summed = lax.dynamic_slice_in_dim(reduced, lax.rem(member, 2) * row_share, row_share, 0)
+    summed = summed[:, :PIX].astype(jnp.float32)
     row_start = member * row_share
     inside_rows = lax.dynamic_slice_in_dim(inside, row_start, row_share, 0)
     grad_latent = jnp.where(inside_rows, summed, 0.0)
-    grad_scale = lsq_factor * lax.dynamic_slice_in_dim(scale_total, row_start, row_share, 0)
+    slope_rows = lax.dynamic_slice_in_dim(scale_slope, row_start, row_share, 0)
+    grad_scale = lsq_factor * jnp.sum(summed * slope_rows, axis=1)
     return (attended, grad_latent, grad_scale)
 
 

time: 521 us -> 179 us (0.34); the launches traced: 512 us -> 178 us
  waiting for transfers between devices: 331 us -> 0 us
  Pallas kernels: 0 us -> 111 us
  blocking collectives: 103 us -> 0 us
  between operations: 14.8 us -> 1.12 us
  matrix products: 37.3 us -> 43.2 us
    all_gather x2 -> x0, waiting for transfers between devices: 173 us -> none  [the longest x1 109 us: per_device(): whole_weight = lax.all_gather(qkv_weight, 'dp', axis=1, tiled=True)]
    psum x1 -> x0, waiting for transfers between devices: 125 us -> none  [per_device(): summed = lax.psum(group_rows, 'dp').astype(jnp.float32)]
    pallas_call x0 -> x2, Pallas kernels: none -> 111 us  [the longest x1 68.9 us: gather_weight(): pl.pallas_call(gather_kernel, name='gather_weight', out_shape=(jax.ShapeD...]
    psum x1 -> x0, blocking collectives: 103 us -> none  [per_device(): lax.psum(jnp.sum(rounded * scale_slope, axis=1), ('dp', 'bal'))]
    unnamed x5 -> x0, waiting for transfers between devices: 34 us -> none
    unnamed x41 -> x59, local copies, waits for them, and re-layouts: 6.42 us -> 12.4 us
    dot_general x3 -> x6, matrix products: 18.9 us -> 19.9 us  [the longest x1 4.9 us: project_backward(): lax.dot_general(one, weight[1], contract, preferred_element_type=jnp.floa...]
  transfers between devices with their start and end apart: 4 -> 0, of which waited for: 4 -> 0; matrix products, arithmetic and copies ran while one was open for 3% -> 0% of each run, Pallas kernels for 0% -> 0%
where the time goes in v1:
time: 179 us; the launch traced here: 178 us
  Pallas kernels  111 us (62%)
  matrix products  43.2 us (24%)
  local copies, waits for them, and re-layouts  12.7 us (7%)
  other arithmetic  10.5 us (6%)
    pallas_call x1, Pallas kernels, gather_weight(): pl.pallas_call(gather_kernel, name='gather_weight', out_shape=(jax.ShapeD...  68.9 us
    pallas_call x1, Pallas kernels, reduce_grad(): pl.pallas_call(reduce_kernel, name='reduce_grad', out_shape=jax.ShapeDtyp...  41.8 us
    unnamed x59, local copies, waits for them, and re-layouts  12.4 us
    dot_general x1, matrix products, forward_backward(): jnp.einsum('hqk,qhd->khd', grad_score, queries, preferred_element_type=jn...  5.69 us
    dot_general x1, matrix products, forward_backward(): jnp.einsum('hqk,khd->qhd', grad_score, key_rows, preferred_element_type=j...  5.01 us
    dot_general x1, matrix products, project_backward(): lax.dot_general(one, weight[1], contract, preferred_element_type=jnp.floa...  4.9 us
    dot_general x1, matrix products, project_forward(): zero = jnp.dot(normed, weight[0], preferred_element_type=jnp.float32)  4.84 us
    dot_general x1, matrix products, project_backward(): lax.dot_general(zero, weight[0], contract, preferred_element_type=jnp.flo...  4.62 us

profile of v1, /device:TPU:1, one launch (start us, length us, event | category | flops | bytes accessed | tf_op | source)
XLA Modules:
  0.0 178.3 jit_solution(369925558665143736)
XLA Ops:
  1.3 0.9 select_reduce_fusion.8
  3.6 0.9 select_reduce_fusion
  4.8 1.3 convolution_convert_fusion.3
  7.2 1.4 copy.36.w_ref
  8.6 68.9 %gather_weight.1 = (bf16[2,1792,1344]{2,1,0:T(8,128)(2,1)S(1)}, bf16[20,32,128]{2,1,0:T(8,128)(2,1)S(1)}) custom-call(bf16[1792,168]{1,0:T(8,128)(2,1)S(1)} %copy.36.w_ref, bf16[20,32,128]{2,1,0:T(8,128)(2,1)S(1)} %bitcast.81, s32[32]{0:T(128)S(1)} %select_reduce_fusion.9.source_ref), custom_call_target="tpu_custom_call" | custom-call | tf_op jit(solution)/shard_map/gather_weight/pallas_call | solution.py:466
  77.5 3.8 %copy-done = bf16[2,1792,1344]{2,1,0:T(8,128)(2,1)} copy-done((bf16[2,1792,1344]{2,1,0:T(8,128)(2,1)}, bf16[2,1792,1344]{2,1,0:T(8,128)(2,1)S(1)}, u32[]{:S(2)}) %copy-start) | copy-done | bytes 9633816
  81.6 1.2 convolution_convert_fusion.2
  82.8 4.3 %copy.38 = bf16[1792,588]{1,0:T(8,128)(2,1)} copy(bf16[1792,588]{0,1:T(8,128)(2,1)} %param.12) | data formatting | bytes 4214784 | tf_op args[1]
  87.1 3.7 %fusion.102 = (f32[256]{0:T(256)S(1)}, f32[256,1792]{1,0:T(8,128)S(1)}) fusion(f32[1792]{0:T(1024)} %param.14, f32[1792]{0:T(1024)S(1)} %copy-done.11, bf16[1792,588]{1,0:T(8,128)(2,1)} %copy.38, bf16[256,640]{1,0:T(8,128)(2,1)} %convolution_convert_fusion.2), kind=kOutput, calls=%fused_computation.149 | convolution fusion | flops 548702976 | bytes 4285440 | tf_op jit(solution)/shard_map/dot_general | solution.py:91
  91.8 3.0 %fusion.7 = bf16[256,1344]{0,1:T(8,128)(2,1)} fusion(bf16[2,1792,1344]{2,1,0:T(8,128)(2,1)S(1)} %bitcast.85, f32[256,1792]{1,0:T(8,128)S(1)} %get-tuple-element.39, f32[1792]{0:T(1024)S(1)} %copy-done.18, f32[1792]{0:T(1024)S(1)} %copy-done.19, f32[256]{0:T(256)S(1)} %add_rsqrt_fusion, f32[256]{0:T(256)S(1)} %broadcast_multiply_fusion.2), kind=kOutput, calls=%fused_computation.7 | convolution fusion | flops 1235419136 | bytes 7587840 | tf_op jit(solution)/shard_map/dot_general | solution.py:812
  94.8 4.8 %select_convert_fusion.1 = (bf16[256,1344]{0,1:T(8,128)(2,1)S(1)}, bf16[256,1344]{0,1:T(8,128)(2,1)S(1)}) fusion(bf16[256,1344]{0,1:T(8,128)(2,1)} %fusion.7, pred[1344]{0:T(1024)(128)(4,1)S(1)} %fusion.79, bf16[2,1792,1344]{2,1,0:T(8,128)(2,1)} %copy-done, f32[256,1792]{1,0:T(8,128)S(1)} %get-tuple-element.39, f32[1792]{0:T(1024)} %param.16, ...), kind=kOutput, calls=%fused_computation.38 | convolution fusion | flops 1236107264 | bytes 8965440 | tf_op jit(solution)/shard_map/dot_general | solution.py:811
  100.0 2.0 %fusion.32 = (f32[8,256]{1,0:T(8,128)S(1)}, f32[8,256,256]{1,2,0:T(8,128)}) fusion(pred[256,256]{0,1:T(8,128)(4,1)S(1)} %and_and_fusion, bf16[256,8,112]{0,2,1:T(8,128)(2,1)S(1)} %bitcast.92, bf16[256,8,112]{0,2,1:T(8,128)(2,1)S(1)} %bitcast.94), kind=kOutput, calls=%fused_computation.37 | convolution fusion | flops 119011328 | bytes 3088384 | tf_op jit(solution)/shard_map/qhd,khd->hqk/dot_general | solution.py:112
  102.0 1.2 copy.40
  103.3 3.0 %convolution_convert_fusion.1 = bf16[8,112,256]{2,1,0:T(8,128)(2,1)} fusion(bf16[256,8,112]{0,2,1:T(8,128)(2,1)S(1)} %bitcast.88, f32[8,256,256]{1,2,0:T(8,128)} %get-tuple-element.41, f32[8,256]{1,0:T(8,128)S(1)} %broadcast_select_fusion, pred[256,256]{0,1:T(8,128)(4,1)S(1)} %and_and_fusion), kind=kOutput, calls=%fused_computation.42 | convolution fusion | flops 119767040 | bytes 3088384 | tf_op jit(solution)/shard_map/hqk,qhd->khd/dot_general | solution.py:128
  106.3 1.8 %fusion.104 = f32[8,256,256]{1,2,0:T(8,128)} fusion(bf16[256,8,112]{0,2,1:T(8,128)(2,1)S(1)} %bitcast.89, bf16[256,8,112]{0,2,1:T(8,128)(2,1)S(1)} %bitcast.86), kind=kOutput, calls=%fused_computation.151 | convolution fusion | flops 117440512 | bytes 3014656 | tf_op jit(solution)/shard_map/qhd,khd->hqk/dot_general | solution.py:131
  108.1 5.0 %fusion.33 = bf16[8,112,256]{2,1,0:T(8,128)(2,1)S(1)} fusion(bf16[256,8,112]{0,2,1:T(8,128)(2,1)} %bitcast.95, f32[8,256,256]{1,2,0:T(8,128)} %fusion.104, f32[8,256,256]{1,2,0:T(8,128)} %get-tuple-element.41, f32[8,256]{1,0:T(8,128)S(1)} %broadcast_select_fusion, pred[256,256]{0,1:T(8,128)(4,1)S(1)} %and_and_fusion), kind=kOutput, calls=%fused_computation.40 | convolution fusion | flops 123439360 | bytes 5185536 | tf_op jit(solution)/shard_map/hqk,khd->qhd/dot_general | solution.py:136
  113.2 5.7 %fusion.36 = bf16[8,112,256]{2,1,0:T(8,128)(2,1)} fusion(bf16[256,8,112]{0,2,1:T(8,128)(2,1)S(1)} %bitcast.93, f32[8,256,256]{1,2,0:T(8,128)} %fusion.104, f32[8,256,256]{1,2,0:T(8,128)} %get-tuple-element.41, f32[8,256]{1,0:T(8,128)S(1)} %broadcast_select_fusion, pred[256,256]{0,1:T(8,128)(4,1)S(1)} %and_and_fusion), kind=kOutput, calls=%fused_computation.41 | convolution fusion | flops 123439360 | bytes 5185536 | tf_op jit(solution)/shard_map/hqk,qhd->khd/dot_general | solution.py:139
  118.9 4.6 %fusion.1 = f32[256,1792]{1,0:T(8,128)S(1)} fusion(bf16[2,1792,1344]{2,1,0:T(8,128)(2,1)} %copy-done, pred[1344]{0:T(1024)(128)(4,1)S(1)} %fusion.79, bf16[256,896]{0,1:T(8,128)(2,1)} %bitcast.107, bf16[256,896]{0,1:T(8,128)(2,1)S(1)} %bitcast.105, bf16[256,896]{0,1:T(8,128)(2,1)S(1)} %bitcast.103), kind=kOutput, calls=%fused_computation.1 | convolution fusion | flops 1236221952 | bytes 8258880 | tf_op jit(solution)/shard_map/dot_general | solution.py:821
  123.6 4.9 %fusion.101 = (f32[256]{0:T(256)S(1)}, f32[256]{0:T(256)S(1)}, f32[256,1792]{1,0:T(8,128)S(1)}) fusion(f32[256]{0:T(256)S(1)} %copy-done.17, f32[256,1792]{1,0:T(8,128)S(1)} %get-tuple-element.39, f32[256]{0:T(256)S(1)} %copy-done.13, f32[1792]{0:T(1024)S(1)} %copy-done.20, f32[256,1792]{1,0:T(8,128)S(1)} %fusion.1, bf16[2,1792,1344]{2,1,0:T(8,128)(2,1)} %copy-done, ...), kind=kOutput, calls=%fused_computation.148 | convolution fusion | flops 1239432704 | bytes 11940160 | tf_op jit(solution)/shard_map/dot_general | solution.py:823
  128.5 1.5 convolution_convert_fusion
  130.0 41.8 %reduce_grad.1 = bf16[7,16,640]{2,1,0:T(8,128)(2,1)S(1)} custom-call(bf16[16,112,640]{2,1,0:T(8,128)(2,1)S(1)} %bitcast.80), custom_call_target="tpu_custom_call" | custom-call | tf_op jit(solution)/shard_map/reduce_grad/pallas_call | solution.py:724
  171.8 1.3 add_floor_fusion
  173.2 2.0 %compare_and_fusion = pred[1792,588]{1,0:T(8,128)(4,1)S(1)} fusion(f32[1792]{0:T(1024)S(1)} %copy-done.11, bf16[1792,588]{1,0:T(8,128)(2,1)S(1)} %copy-done.1), kind=kLoop, calls=%fused_computation.12 | loop fusion | flops 7375872 | bytes 3168256 | tf_op jit(solution)/shard_map/and | solution.py:24
  177.4 1.0 copy.44
  (82 shorter events, 7.1 us)
Async XLA Ops:
  6.1 75.4 %copy-start.4 = (bf16[320,588]{1,0:T(8,128)(2,1)S(1)}, bf16[320,588]{1,0:T(8,128)(2,1)}, u32[]{:S(2)}) copy-start(bf16[320,588]{1,0:T(8,128)(2,1)} %param.11) | copy-start | bytes 1128964
  77.5 3.8 %copy-start = (bf16[2,1792,1344]{2,1,0:T(8,128)(2,1)}, bf16[2,1792,1344]{2,1,0:T(8,128)(2,1)S(1)}, u32[]{:S(2)}) copy-start(bf16[2,1792,1344]{2,1,0:T(8,128)(2,1)S(1)} %get-tuple-element.6) | copy-start | bytes 28901380
  82.8 4.3 %copy-start.11 = (f32[1792]{0:T(1024)S(1)}, f32[1792]{0:T(1024)}, u32[]{:S(2)}) copy-start(f32[1792]{0:T(1024)} %param.13) | copy-start | bytes 21508
  82.8 8.9 %slice-start = ((s8[10092544]{0:T(1024)(128)(4,1)}), s8[1703936]{0:T(1024)(128)(4,1)S(1)}, s32[]{:S(2)}) async-start(s8[10092544]{0:T(1024)(128)(4,1)} %bitcast.84), calls=%async_computation | async-start | bytes 3407872
  87.1 4.7 %slice-start.1 = ((s8[10092544]{0:T(1024)(128)(4,1)}), s8[4194304]{0:T(1024)(128)(4,1)S(1)}, s32[]{:S(2)}) async-start(s8[10092544]{0:T(1024)(128)(4,1)} %bitcast.84), calls=%async_computation.1 | async-start | bytes 8388608
  87.1 4.7 %slice-start.2 = ((s8[10092544]{0:T(1024)(128)(4,1)}), s8[4194304]{0:T(1024)(128)(4,1)S(1)}, s32[]{:S(2)}) async-start(s8[10092544]{0:T(1024)(128)(4,1)} %bitcast.84), calls=%async_computation.2 | async-start | bytes 8388608
  87.1 4.7 %copy-start.18 = (f32[1792]{0:T(1024)S(1)}, f32[1792]{0:T(1024)}, u32[]{:S(2)}) copy-start(f32[1792]{0:T(1024)} %param.16) | copy-start | bytes 21508
  87.1 4.7 %copy-start.19 = (f32[1792]{0:T(1024)S(1)}, f32[1792]{0:T(1024)}, u32[]{:S(2)}) copy-start(f32[1792]{0:T(1024)} %param.15) | copy-start | bytes 21508
  99.8 2.2 %copy-start.7 = (bf16[256,896]{0,1:T(8,128)(2,1)}, bf16[256,896]{0,1:T(8,128)(2,1)S(1)}, u32[]{:S(2)}) copy-start(bf16[256,896]{0,1:T(8,128)(2,1)S(1)} %get-tuple-element.30) | copy-start | bytes 1376260
  99.8 6.5 %copy-start.2 = (bf16[256,896]{0,1:T(8,128)(2,1)}, bf16[256,896]{0,1:T(8,128)(2,1)S(1)}, u32[]{:S(2)}) copy-start(bf16[256,896]{0,1:T(8,128)(2,1)S(1)} %get-tuple-element.32) | copy-start | bytes 1376260
  99.9 13.2 %copy-start.9 = (pred[256,256]{0,1:T(8,128)(4,1)}, pred[256,256]{0,1:T(8,128)(4,1)S(1)}, u32[]{:S(2)}) copy-start(pred[256,256]{0,1:T(8,128)(4,1)S(1)} %and_and_fusion) | copy-start | bytes 196612
  102.0 11.2 %copy-start.14 = (f32[8,256]{1,0:T(8,128)}, f32[8,256]{1,0:T(8,128)S(1)}, u32[]{:S(2)}) copy-start(f32[8,256]{1,0:T(8,128)S(1)} %broadcast_select_fusion) | copy-start | bytes 24580
  108.1 5.0 %copy-start.6 = (bf16[256,896]{0,1:T(8,128)(2,1)S(1)}, bf16[256,896]{0,1:T(8,128)(2,1)}, u32[]{:S(2)}) copy-start(bf16[256,896]{0,1:T(8,128)(2,1)} %copy-done.5) | copy-start | bytes 1376260
  113.2 5.7 %copy-start.21 = (bf16[8,112,256]{2,1,0:T(8,128)(2,1)S(1)}, bf16[8,112,256]{2,1,0:T(8,128)(2,1)}, u32[]{:S(2)}) copy-start(bf16[8,112,256]{2,1,0:T(8,128)(2,1)} %convolution_convert_fusion.1) | copy-start | bytes 1376260
  118.9 4.7 %copy-start.13 = (f32[256]{0:T(256)S(1)}, f32[256]{0:T(256)}, u32[]{:S(2)}) copy-start(f32[256]{0:T(256)} %copy-done.12) | copy-start | bytes 3076
  118.9 4.7 %copy-start.17 = (f32[256]{0:T(256)S(1)}, f32[256]{0:T(256)}, u32[]{:S(2)}) copy-start(f32[256]{0:T(256)} %copy-done.16) | copy-start | bytes 3076
  118.9 4.7 %copy-start.20 = (f32[1792]{0:T(1024)S(1)}, f32[1792]{0:T(1024)}, u32[]{:S(2)}) copy-start(f32[1792]{0:T(1024)} %param.15) | copy-start | bytes 21508
  118.9 4.7 %copy-start.22 = (bf16[8,112,256]{2,1,0:T(8,128)(2,1)S(1)}, bf16[8,112,256]{2,1,0:T(8,128)(2,1)}, u32[]{:S(2)}) copy-start(bf16[8,112,256]{2,1,0:T(8,128)(2,1)} %fusion.36) | copy-start | bytes 1376260
  123.6 4.9 %copy-start.8 = (bf16[256,640]{1,0:T(8,128)(2,1)S(1)}, bf16[256,640]{1,0:T(8,128)(2,1)}, u32[]{:S(2)}) copy-start(bf16[256,640]{1,0:T(8,128)(2,1)} %convolution_convert_fusion.2) | copy-start | bytes 983044
  130.0 41.9 %copy-start.1 = (bf16[1792,588]{1,0:T(8,128)(2,1)S(1)}, bf16[1792,588]{1,0:T(8,128)(2,1)}, u32[]{:S(2)}) copy-start(bf16[1792,588]{1,0:T(8,128)(2,1)} %copy.38) | copy-start | bytes 6322180
  173.2 3.4 %copy-start.3 = (bf16[256,896]{0,1:T(8,128)(2,1)S(1)}, bf16[256,896]{0,1:T(8,128)(2,1)}, u32[]{:S(2)}) copy-start(bf16[256,896]{0,1:T(8,128)(2,1)} %copy-done.2) | copy-start | bytes 1376260
  173.2 3.4 %copy-start.10 = (pred[256,256]{0,1:T(8,128)(4,1)S(1)}, pred[256,256]{0,1:T(8,128)(4,1)}, u32[]{:S(2)}) copy-start(pred[256,256]{0,1:T(8,128)(4,1)} %copy-done.9) | copy-start | bytes 196612
  173.2 3.3 %copy-start.15 = (f32[8,256]{1,0:T(8,128)S(1)}, f32[8,256]{1,0:T(8,128)}, u32[]{:S(2)}) copy-start(f32[8,256]{1,0:T(8,128)} %copy-done.14) | copy-start | bytes 24580
  173.2 3.3 %copy-start.23 = (f32[8,256,256]{1,2,0:T(8,128)S(1)}, f32[8,256,256]{1,2,0:T(8,128)}, u32[]{:S(2)}) copy-start(f32[8,256,256]{1,2,0:T(8,128)} %get-tuple-element.41) | copy-start | bytes 6291460
  (3 other events, 3.3 us)

commit v2 on v1

v2 whole, which is shorter than its diff:
```python
import math

import jax
import jax.numpy as jnp
from jax import lax
from jax.experimental import pallas as pl
from jax.experimental.pallas import tpu as pltpu
from jax.sharding import PartitionSpec as P

D = 1792
HEAD = 112
PIX = 588
HEADS = 8
MOVE_ROWS = 128
EPSILON = 1e-06
MESH = pl.DeviceIdType.MESH
SHARD = 168
MAIN = 128
REST_PAD = 48
CHIP_ROWS = 112
PIX_PAD = 640
PIECES = 20


def place():
    z = lax.axis_index("dp")
    b = lax.axis_index("bal")
    core = lax.rem(b, 2)
    x = lax.rem(b // 2, 4)
    y = b // 8
    return z, b, x, y, core


def remote(src, dst, send, recv, device):
    copy = pltpu.make_async_remote_copy(
        src_ref=src, dst_ref=dst, send_sem=send, recv_sem=recv, device_id=device, device_id_type=MESH
    )
    return copy


def gather_kernel(
    w_ref,
    latent_ref,
    scale_ref,
    bias_ref,
    gain_ref,
    shift_ref,
    pixels_ref,
    length_ref,
    source_ref,
    target_ref,
    sender_ref,
    main_out,
    rest_out,
    moved_ref,
    embedded_ref,
    projected_ref,
    column_id_ref,
    row_id_ref,
    main,
    rest,
    rows_in,
    pieces,
    inbox,
    stage,
    arrived,
    quant,
    normed,
    part_main,
    part_rest,
    z_send,
    z_recv,
    ring_send,
    ring_recv,
    hand_send,
    hand_recv,
    out_send,
    out_recv,
    back_send,
    back_recv,
    plane_send,
    plane_recv,
    pair_send,
    pair_recv,
    save_sem,
):
    z, b, x, y, core = place()
    sibling = b + 1 - 2 * core
    chip = b // 2
    quad = z // 4
    barrier = pltpu.get_barrier_semaphore()

    def greet_plane(step, carry):
        pl.semaphore_signal(
            barrier, inc=1, device_id=(z, lax.rem(b + step, 32)), device_id_type=MESH
        )
        return carry

    def greet_line(step, carry):
        pl.semaphore_signal(
            barrier, inc=1, device_id=(lax.rem(z + step, 16), b), device_id_type=MESH
        )
        return carry

    lax.fori_loop(1, 16, greet_line, 0)
    lax.fori_loop(1, 32, greet_plane, 0)

    def slice_rows(where):
        return pl.ds(pl.multiple_of((where // 2) * 16, 16), 16)

    def slice_lanes(where):
        return pl.ds(pl.multiple_of(lax.rem(where, 2) * 896, 128), 896)

    @pl.when(core == 0)
    def _():
        main[z, slice_rows(chip), slice_lanes(chip)] = w_ref[slice_rows(chip), slice_lanes(chip)]

    def rest_rows(plane):
        return pl.ds(pl.multiple_of(plane * REST_PAD, 16), REST_PAD)

    rest[rest_rows(z), :] = jnp.concatenate(
        [w_ref[pl.ds(MAIN, SHARD - MAIN), :], jnp.zeros((REST_PAD - SHARD + MAIN, D), jnp.bfloat16)],
        axis=0,
    )
    pl.semaphore_wait(barrier, 46)

    def z_copy(step):
        to = lax.rem(z + step, 16)
        return remote(
            w_ref.at[slice_rows(chip), slice_lanes(chip)],
            main.at[z, slice_rows(chip), slice_lanes(chip)],
            z_send.at[step],
            z_recv.at[z],
            (to, b),
        )

    def z_mine(step):
        return lax.rem(lax.rem(z + step, 16) // 4 + quad, 2) == core

    for step in (1, 15, 2, 14, 3, 13, 4, 12, 5, 11, 6, 10, 7, 9, 8):

        @pl.when(z_mine(step))
        def _():
            z_copy(step).start()

    def half_lanes(which, part):
        start, count = ((0, 512), (512, 384))[part]
        return pl.ds(pl.multiple_of(which * 896 + start, 128), count)

    def ring_copy(way, step, part):
        sign = 1 if way == 0 else -1
        origin = lax.rem(z - sign * (step - 1) + 16, 16)
        to = lax.rem(z + sign + 16, 16)
        block = rest.at[rest_rows(origin), half_lanes(core, part)]
        return remote(
            block, block, ring_send.at[way, step, part], ring_recv.at[way, step, part], (to, b)
        )

    def ring_wait(way, step, part):
        sign = 1 if way == 0 else -1
        origin = lax.rem(z - sign * step + 16, 16)
        block = rest.at[rest_rows(origin), half_lanes(core, part)]
        remote(
            block,
            block,
            ring_send.at[way, step, part],
            ring_recv.at[way, step, part],
            (lax.rem(z + 1, 16), b),
        ).wait_recv()

    def hand_copy(which, way, step):
        sign = 1 if way == 0 else -1
        origin = lax.rem(z - sign * step + 16, 16)
        block = rest.at[
            rest_rows(origin), pl.ds(pl.multiple_of(which * 896, 128), 896)
        ]
        return remote(
            block, block, hand_send.at[way, step], hand_recv.at[way, step], (z, sibling)
        )

    last = (8, 7)
    for part in range(2):
        for way in range(2):
            ring_copy(way, 1, part).start()

    def ring_step(step):
        for part in range(2):
            for way in range(2):
                if step <= last[way]:
                    ring_wait(way, step, part)
                    if step < last[way]:
                        ring_copy(way, step + 1, part).start()
        for way in range(2):
            if step <= last[way]:
                hand_copy(core, way, step).start()

    length_row = length_ref[...].astype(jnp.float32)
    source_row = source_ref[...].astype(jnp.float32)
    target_row = target_ref[...].astype(jnp.float32)
    entries = length_row.shape[1]

    def turned(row):
        return jnp.broadcast_to(row, (entries, entries)).T

    length_col, source_col, target_col = turned(length_row), turned(source_row), turned(target_row)
    down = lax.broadcasted_iota(jnp.int32, (entries, entries), 0)
    along = lax.broadcasted_iota(jnp.int32, (entries, entries), 1)
    member = b.astype(jnp.float32)

    def above(owner_col, owner_row, amount_col):
        match = (down < along) & (owner_col == owner_row)
        return jnp.sum(jnp.where(match, amount_col, 0.0), axis=0, keepdims=True)

    target_start = above(target_col, target_row, length_col)
    source_start = above(source_col, source_row, length_col)
    moving_col = jnp.where(target_col != source_col, length_col, 0.0)
    outbox_start = above(source_col, source_row, moving_col)
    before = (along < down) & (target_col == target_row)
    target_start_col = jnp.sum(jnp.where(before, length_row, 0.0), axis=1, keepdims=True)

    slots = lax.broadcasted_iota(jnp.int32, (MOVE_ROWS, entries), 0).astype(jnp.float32)
    leaving = (
        (source_row == member)
        & (target_row != source_row)
        & (slots >= outbox_start)
        & (slots < outbox_start + length_row)
    )
    leaving_row = jnp.sum(
        jnp.where(leaving, source_start - outbox_start + slots, 0.0), axis=1, keepdims=True
    )
    leaving_any = jnp.sum(jnp.where(leaving, 1.0, 0.0), axis=1, keepdims=True)
    leaving_row = jnp.where(leaving_any > 0.0, leaving_row, -1.0)
    count_in = pixels_ref.shape[0]
    rows_in[:, pl.ds(512, 128)] = jnp.zeros((rows_in.shape[0], 128), jnp.bfloat16)
    rows_in[pl.ds(0, count_in), pl.ds(0, PIX)] = pixels_ref[...]
    picks = lax.broadcasted_iota(jnp.int32, (MOVE_ROWS, count_in), 1).astype(jnp.float32)
    outgoing = jnp.dot(
        jnp.where(leaving_row == picks, 1.0, 0.0).astype(jnp.bfloat16),
        rows_in[pl.ds(0, count_in), :],
        preferred_element_type=jnp.float32,
    ).astype(jnp.bfloat16)
    for i in range(4):
        for j in range(5):
            pieces[5 * i + j] = outgoing[32 * i : 32 * i + 32, 128 * j : 128 * j + 128]

    def out_copy(target, slot):
        return remote(
            pieces.at[target], inbox.at[slot], out_send.at[target], out_recv.at[slot], (z, target)
        )

    def back_copy(target, slot):
        return remote(
            stage.at[target], arrived.at[slot], back_send.at[target], back_recv.at[slot], (z, target)
        )

    def send_out(step, carry):
        target = lax.rem(b + step, 32)

        @pl.when(target < PIECES)
        def _():
            out_copy(target, b).start()

        return carry

    lax.fori_loop(1, 32, send_out, 0)

    def quad_of(which, chunk):
        base = quad * (1 - which) + which * (quad + 3 + 2 * (lax.rem(z, 4) // 2))
        return lax.rem(base + 2 * chunk, 4)

    def chip_at(which, chunk, first, second):
        swap = lax.rem(which + chunk, 2)
        dx = first * (1 - swap) + second * swap
        dy = first * swap + second * (1 - swap)
        return lax.rem(y + dy + 4, 4) * 4 + lax.rem(x + dx + 4, 4)

    def piece(which, chunk, where, low=0, count=4):
        return main.at[
            pl.ds(4 * quad_of(which, chunk) + low, count), slice_rows(where), slice_lanes(where)
        ]

    offsets = (0, -1, 1, 2)
    spans = ((0, 4), (0, 4), (0, 2), (2, 2))

    def hop(chunk, index, axis, place_index, kind):
        low, count = spans[kind]
        sign = 1 if kind in (0, 2) else -1
        origin = (0, 0, -1, 1)[kind]
        a = offsets[place_index]
        if axis == 0:
            to, sent = chip_at(core, chunk, sign, 0), chip_at(core, chunk, origin, 0)
        else:
            to, sent = chip_at(core, chunk, 0, sign), chip_at(core, chunk, a, origin)
        rows = piece(core, chunk, sent, low, count)
        return remote(
            rows, rows, plane_send.at[chunk, index], plane_recv.at[chunk, index], (z, to * 2 + core)
        )

    def hop_wait(chunk, index, axis, place_index, kind):
        low, count = spans[kind]
        origin = (-1, 1, 2, 2)[kind]
        a = offsets[place_index]
        if axis == 0:
            sent = chip_at(core, chunk, origin, 0)
        else:
            sent = chip_at(core, chunk, a, origin)
        rows = piece(core, chunk, sent, low, count)
        remote(
            rows, rows, plane_send.at[chunk, index], plane_recv.at[chunk, index], (z, sibling)
        ).wait_recv()

    def first_copy(chunk, kind):
        return hop(chunk, kind, 0, 0, kind)

    def first_wait(chunk, kind):
        hop_wait(chunk, kind, 0, 0, kind)

    def second_copy(chunk, place_index, kind):
        return hop(chunk, 4 + 4 * place_index + kind, 1, place_index, kind)

    def second_wait(chunk, place_index, kind):
        hop_wait(chunk, 4 + 4 * place_index + kind, 1, place_index, kind)

    def pair_copy(which, chunk, place_index, second_index):
        rows = piece(
            which, chunk, chip_at(which, chunk, offsets[place_index], offsets[second_index])
        )
        index = place_index * 4 + second_index
        return remote(
            rows, rows, pair_send.at[chunk, index], pair_recv.at[chunk, index], (z, sibling)
        )

    def chunk_start(chunk):
        for j in range(4):
            origin = 4 * quad_of(core, chunk) + j

            @pl.when(origin != z)
            def _():
                rows = main.at[origin, slice_rows(chip), slice_lanes(chip)]
                remote(rows, rows, z_send.at[0], z_recv.at[origin], (z, sibling)).wait_recv()

        first_copy(chunk, 0).start()
        first_copy(chunk, 1).start()
        second_copy(chunk, 0, 0).start()
        second_copy(chunk, 0, 1).start()
        pair_copy(core, chunk, 0, 0).start()

    def chunk_first(chunk):
        for kind, index in ((0, 1), (1, 2)):
            first_wait(chunk, kind)
            first_copy(chunk, kind + 2).start()
            second_copy(chunk, index, 0).start()
            second_copy(chunk, index, 1).start()
            pair_copy(core, chunk, index, 0).start()

    def chunk_far(chunk):
        first_wait(chunk, 2)
        first_wait(chunk, 3)
        second_copy(chunk, 3, 0).start()
        second_copy(chunk, 3, 1).start()
        pair_copy(core, chunk, 3, 0).start()

    def chunk_second(chunk, index):
        for kind in (0, 1):
            second_wait(chunk, index, kind)
            second_copy(chunk, index, kind + 2).start()
            pair_copy(core, chunk, index, kind + 1).start()

    def chunk_last(chunk, index):
        second_wait(chunk, index, 2)
        second_wait(chunk, index, 3)
        pair_copy(core, chunk, index, 3).start()

    def quantize_part(part, carry):
        lanes = pl.ds(pl.multiple_of(part * 256, 128), 256)
        scale = scale_ref[:, lanes]
        level = jnp.floor(latent_ref[:, lanes].astype(jnp.float32) / scale + 0.5)
        quant[pl.ds(0, PIX), lanes] = (jnp.clip(level, -8.0, 7.0) * scale).astype(jnp.bfloat16)
        return carry

    def embed_part(part, carry):
        lanes = pl.ds(pl.multiple_of(part * 256, 128), 256)
        total = jnp.dot(moved_ref[...], quant[:, lanes], preferred_element_type=jnp.float32)
        embedded_ref[:, lanes] = (total + bias_ref[:, lanes]).astype(jnp.bfloat16)
        return carry

    def norm_part(part, carry):
        rows = pl.ds(pl.multiple_of(part * 32, 32), 32)
        values = embedded_ref[rows, :].astype(jnp.float32)
        centered = values - jnp.mean(values, axis=1, keepdims=True)
        variance = jnp.mean(centered * centered, axis=1, keepdims=True)
        hat = centered * lax.rsqrt(variance + EPSILON)
        normed[rows, :] = (hat * gain_ref[...] + shift_ref[...]).astype(jnp.bfloat16)
        return carry

    chunk_start(0)
    ring_step(1)

    @pl.when(b < PIECES)
    def _():
        inbox[b] = pieces[b]

        def take(step, carry):
            out_copy(b, lax.rem(b + step, 32)).wait_recv()
            return carry

        lax.fori_loop(1, 32, take, 0)
        arrived[b] = inbox[sender_ref[b]]

        def send_back(step, carry):
            target = lax.rem(b + step, 32)
            stage[target] = inbox[sender_ref[target]]
            back_copy(target, b).start()
            return carry

        lax.fori_loop(1, 32, send_back, 0)

    chunk_first(0)
    ring_step(2)
    quant[pl.ds(576, 64), :] = jnp.zeros((64, D), jnp.bfloat16)
    lax.fori_loop(0, 7, quantize_part, 0)
    chunk_far(0)
    chunk_second(0, 0)
    ring_step(3)

    row = lax.broadcasted_iota(jnp.int32, (moved_ref.shape[0], entries), 0).astype(jnp.float32)
    covers = (target_row == member) & (row >= target_start) & (row < target_start + length_row)
    take_from = (
        jnp.where(source_row == member, source_start, outbox_start + float(count_in)) - target_start
    )
    wanted = jnp.sum(jnp.where(covers, take_from + row, 0.0), axis=1, keepdims=True)
    entry = (lax.broadcasted_iota(jnp.int32, (1, entries), 1) + 1).astype(jnp.float32)
    image = jnp.sum(jnp.where(covers, entry, 0.0), axis=1, keepdims=True)
    wanted = jnp.where(image > 0.0, wanted, -1.0)
    column_id_ref[...] = image
    across = lax.broadcasted_iota(jnp.int32, (entries, moved_ref.shape[0]), 1).astype(jnp.float32)
    covers_turned = (
        (target_col[:, :1] == member)
        & (across >= target_start_col)
        & (across < target_start_col + length_col[:, :1])
    )
    entry_down = (lax.broadcasted_iota(jnp.int32, (entries, 1), 0) + 1).astype(jnp.float32)
    row_id_ref[...] = jnp.sum(jnp.where(covers_turned, entry_down, 0.0), axis=0, keepdims=True)

    def arrive(step, carry):
        slot = lax.rem(b + step, 32)

        @pl.when(slot < PIECES)
        def _():
            back_copy(b, slot).wait_recv()

        return carry

    lax.fori_loop(1, 32, arrive, 0)
    for i in range(4):
        for j in range(5):
            rows_in[pl.ds(count_in + 32 * i, 32), pl.ds(128 * j, 128)] = arrived[5 * i + j]
    choose = lax.broadcasted_iota(
        jnp.int32, (moved_ref.shape[0], count_in + MOVE_ROWS), 1
    ).astype(jnp.float32)
    moved_ref[...] = jnp.dot(
        jnp.where(wanted == choose, 1.0, 0.0).astype(jnp.bfloat16),
        rows_in[...],
        preferred_element_type=jnp.float32,
    ).astype(jnp.bfloat16)
    chunk_second(0, 1)
    chunk_start(1)
    ring_step(4)
    lax.fori_loop(0, 4, embed_part, 0)
    chunk_second(0, 2)
    chunk_first(1)
    ring_step(5)
    lax.fori_loop(4, 7, embed_part, 0)
    chunk_second(0, 3)
    chunk_far(1)
    chunk_second(1, 0)
    ring_step(6)
    lax.fori_loop(0, 4, norm_part, 0)
    chunk_second(1, 1)
    chunk_second(1, 2)
    ring_step(7)
    lax.fori_loop(4, 8, norm_part, 0)
    chunk_second(1, 3)
    for index in range(4):
        chunk_last(0, index)
    ring_step(8)
    for index in range(4):
        chunk_last(1, index)

    def project(which, chunk):
        q = quad_of(which, chunk)
        for pair in range(2):
            block = main[pl.ds(4 * q + 2 * pair, 2)].reshape(256, D)
            part_main[4 * q // 2 + pair] = lax.dot_general(
                normed[...], block, (((1,), (1,)), ((), ())), preferred_element_type=jnp.float32
            ).astype(jnp.bfloat16)

    def pair_wait(chunk):
        for index in range(4):
            for second in range(4):
                pair_copy(1 - core, chunk, index, second).wait_recv()

    project(core, 0)
    pair_wait(0)
    project(1 - core, 0)
    project(core, 1)
    pair_wait(1)
    save_main = pltpu.make_async_copy(main, main_out, save_sem.at[0])
    save_main.start()
    project(1 - core, 1)
    for way in range(2):
        for step in range(1, last[way] + 1):
            hand_copy(1 - core, way, step).wait_recv()
    save_rest = pltpu.make_async_copy(rest, rest_out, save_sem.at[1])
    save_rest.start()
    for part in range(3):
        part_rest[:, 256 * part : 256 * part + 256] = lax.dot_general(
            normed[...],
            rest[pl.ds(256 * part, 256), :],
            (((1,), (1,)), ((), ())),
            preferred_element_type=jnp.float32,
        ).astype(jnp.bfloat16)
    joined = []
    for plane in range(16):
        joined.append(part_main[plane // 2, :, 128 * (plane % 2) : 128 * (plane % 2) + 128])
        joined.append(part_rest[:, REST_PAD * plane : REST_PAD * plane + SHARD - MAIN])
    projected_ref[...] = jnp.concatenate(joined, axis=1)

    for step in range(1, 16):

        @pl.when(z_mine(step))
        def _():
            z_copy(step).wait_send()

    for way in range(2):
        for step in range(1, last[way] + 1):
            for part in range(2):
                ring_copy(way, step, part).wait_send()
            hand_copy(core, way, step).wait_send()

    def sent_out(step, carry):
        target = lax.rem(b + step, 32)

        @pl.when(target < PIECES)
        def _():
            out_copy(target, b).wait_send()

        return carry

    lax.fori_loop(1, 32, sent_out, 0)

    @pl.when(b < PIECES)
    def _():
        def sent_back(step, carry):
            back_copy(lax.rem(b + step, 32), b).wait_send()
            return carry

        lax.fori_loop(1, 32, sent_back, 0)

    for chunk in range(2):
        for kind in range(4):
            first_copy(chunk, kind).wait_send()
            for index in range(4):
                second_copy(chunk, index, kind).wait_send()
        for index in range(4):
            for second in range(4):
                pair_copy(core, chunk, index, second).wait_send()
    save_main.wait()
    save_rest.wait()


def gather_project(weight, latent, scale, bias, gain, shift, pixels, length, source, target, sender):
    vmem = pl.BlockSpec(memory_space=pltpu.VMEM)
    anywhere = pl.BlockSpec(memory_space=pl.ANY)
    dma = pltpu.SemaphoreType.DMA
    rows = 256
    shape = jax.ShapeDtypeStruct
    return pl.pallas_call(
        gather_kernel,
        name="gather_project",
        out_shape=(
            shape((16, MAIN, D), jnp.bfloat16),
            shape((16 * REST_PAD, D), jnp.bfloat16),
            shape((rows, PIX_PAD), jnp.bfloat16),
            shape((rows, D), jnp.bfloat16),
            shape((rows, 16 * SHARD), jnp.bfloat16),
            shape((rows, 1), jnp.float32),
            shape((1, rows), jnp.float32),
        ),
        in_specs=[vmem] * 10 + [pl.BlockSpec(memory_space=pltpu.SMEM)],
        out_specs=(anywhere, anywhere, vmem, vmem, vmem, vmem, vmem),
        scratch_shapes=[
            pltpu.VMEM((16, MAIN, D), jnp.bfloat16),
            pltpu.VMEM((16 * REST_PAD, D), jnp.bfloat16),
            pltpu.VMEM((pixels.shape[0] + MOVE_ROWS, PIX_PAD), jnp.bfloat16),
            pltpu.VMEM((PIECES, 32, 128), jnp.bfloat16),
            pltpu.VMEM((32, 32, 128), jnp.bfloat16),
            pltpu.VMEM((32, 32, 128), jnp.bfloat16),
            pltpu.VMEM((PIECES, 32, 128), jnp.bfloat16),
            pltpu.VMEM((PIX_PAD, D), jnp.bfloat16),
            pltpu.VMEM((rows, D), jnp.bfloat16),
            pltpu.VMEM((8, rows, 256), jnp.bfloat16),
            pltpu.VMEM((rows, 16 * REST_PAD), jnp.bfloat16),
            dma((16,)),
            dma((16,)),
            dma((2, 9, 2)),
            dma((2, 9, 2)),
            dma((2, 9)),
            dma((2, 9)),
            dma((32,)),
            dma((32,)),
            dma((32,)),
            dma((32,)),
            dma((2, 20)),
            dma((2, 20)),
            dma((2, 16)),
            dma((2, 16)),
            dma((2,)),
        ],
        compiler_params=pltpu.CompilerParams(
            collective_id=0, has_side_effects=True, vmem_limit_bytes=48 * 1024 * 1024
        ),
    )(weight, latent, scale, bias, gain, shift, pixels, length, source, target, sender)


def attention_kernel(
    projected_ref,
    column_id_ref,
    row_id_ref,
    cotangent_ref,
    embedded_ref,
    gain_ref,
    moved_ref,
    main_in,
    rest_in,
    attended_ref,
    grad_ref,
    main,
    rest,
    grad_out,
    attended,
    grad_projected,
    grad_main,
    grad_rest,
    grad_normed,
    grad_embedded,
    load_sem,
):
    load_main = pltpu.make_async_copy(main_in, main, load_sem.at[0])
    load_rest = pltpu.make_async_copy(rest_in, rest, load_sem.at[1])
    load_main.start()
    load_rest.start()
    width = HEADS * HEAD
    score_scale = HEAD ** (-0.5)
    grad_factor = 1.0 / math.sqrt(131072.0)
    column_id = column_id_ref[...]
    row_id = row_id_ref[...]
    active = column_id > 0.0
    same = (column_id == row_id) & active
    grad_out[...] = jnp.where(
        active, cotangent_ref[...].astype(jnp.float32) * grad_factor, 0.0
    ).astype(jnp.bfloat16)
    attended[...] = jnp.zeros_like(attended)
    grad_projected[...] = jnp.zeros_like(grad_projected)
    by_rows = (((1,), (1,)), ((), ()))
    by_columns = (((0,), (0,)), ((), ()))

    def dot(left, right, contract=(((1,), (0,)), ((), ()))):
        return lax.dot_general(left, right, contract, preferred_element_type=jnp.float32)

    for head in range(HEADS):
        start = HEAD * head // 128 * 128
        stop = -(-(HEAD * head + HEAD) // 128) * 128
        span = stop - start
        lane = lax.broadcasted_iota(jnp.int32, (1, span), 1) + start
        own = (lane >= HEAD * head) & (lane < HEAD * head + HEAD)

        def window(ref, base=0):
            return ref[:, base + start : base + stop]

        def masked(value):
            return jnp.where(own, value, jnp.zeros_like(value))

        queries, keys, values = (window(projected_ref, width * i) for i in range(3))
        out = window(grad_out)
        keys, values = masked(keys), masked(values)
        scores = dot(queries, keys, by_rows) * score_scale
        exponent = jnp.where(same, jnp.exp(scores), 0.0)
        total = jnp.sum(exponent, axis=1, keepdims=True)
        attention = exponent / jnp.where(active, total, 1.0)
        soft = attention.astype(jnp.bfloat16)
        attended[:, start:stop] += dot(soft, values)
        grad_attention = dot(out, values, by_rows)
        inner = jnp.sum(attention * grad_attention, axis=1, keepdims=True)
        grad_score = (attention * (grad_attention - inner) * score_scale).astype(jnp.bfloat16)
        grad_projected[:, start:stop] += dot(grad_score, keys)
        grad_projected[:, width + start : width + stop] += dot(
            grad_score, masked(queries), by_columns
        )
        grad_projected[:, 2 * width + start : 2 * width + stop] += dot(
            soft, masked(out), by_columns
        )
    attended_ref[...] = attended[...].astype(jnp.bfloat16)
    rounded = grad_projected[...].astype(jnp.bfloat16)
    pad = jnp.zeros((rounded.shape[0], REST_PAD - SHARD + MAIN), jnp.bfloat16)
    mains, rests = [], []
    for plane in range(16):
        base = SHARD * plane
        mains.append(rounded[:, base : base + MAIN])
        rests.append(rounded[:, base + MAIN : base + SHARD])
        rests.append(pad)
    grad_main[...] = jnp.concatenate(mains, axis=1)
    grad_rest[...] = jnp.concatenate(rests, axis=1)
    load_main.wait()
    load_rest.wait()

    def back_part(part, carry):
        lanes = pl.ds(pl.multiple_of(part * 256, 128), 256)
        grad_normed[:, lanes] = dot(
            grad_main[...], main[:, :, lanes].reshape(16 * MAIN, 256)
        ) + dot(grad_rest[...], rest[:, lanes])
        return carry

    lax.fori_loop(0, 7, back_part, 0)

    def norm_part(part, carry):
        rows = pl.ds(pl.multiple_of(part * 32, 32), 32)
        values = embedded_ref[rows, :].astype(jnp.float32)
        centered = values - jnp.mean(values, axis=1, keepdims=True)
        variance = jnp.mean(centered * centered, axis=1, keepdims=True)
        inverse = lax.rsqrt(variance + EPSILON)
        hat = centered * inverse
        gained = grad_normed[rows, :] * gain_ref[...]
        result = inverse * (
            gained
            - jnp.mean(gained, axis=1, keepdims=True)
            - hat * jnp.mean(gained * hat, axis=1, keepdims=True)
        )
        grad_embedded[rows, :] = jnp.where(column_id_ref[rows, :] > 0.0, result, 0.0).astype(
            jnp.bfloat16
        )
        return carry

    lax.fori_loop(0, 8, norm_part, 0)
    for part in range(2):
        block = dot(grad_embedded[:, 896 * part : 896 * part + 896], moved_ref[...], by_columns)
        grad_ref[8 * part : 8 * part + 8] = block.astype(jnp.bfloat16).reshape(
            8, CHIP_ROWS, PIX_PAD
        )


def attend(projected, column_id, row_id, cotangent, embedded, gain, moved, main, rest):
    vmem = pl.BlockSpec(memory_space=pltpu.VMEM)
    anywhere = pl.BlockSpec(memory_space=pl.ANY)
    rows = projected.shape[0]
    shape = jax.ShapeDtypeStruct
    return pl.pallas_call(
        attention_kernel,
        name="attend",
        out_shape=(
            shape((rows, HEADS * HEAD), jnp.bfloat16),
            shape((D // CHIP_ROWS, CHIP_ROWS, PIX_PAD), jnp.bfloat16),
        ),
        in_specs=[vmem] * 7 + [anywhere] * 2,
        out_specs=(vmem, vmem),
        scratch_shapes=[
            pltpu.VMEM((16, MAIN, D), jnp.bfloat16),
            pltpu.VMEM((16 * REST_PAD, D), jnp.bfloat16),
            pltpu.VMEM((rows, HEADS * HEAD), jnp.bfloat16),
            pltpu.VMEM((rows, HEADS * HEAD), jnp.float32),
            pltpu.VMEM((rows, 16 * SHARD), jnp.float32),
            pltpu.VMEM((rows, 16 * MAIN), jnp.bfloat16),
            pltpu.VMEM((rows, 16 * REST_PAD), jnp.bfloat16),
            pltpu.VMEM((rows, D), jnp.float32),
            pltpu.VMEM((rows, D), jnp.bfloat16),
            pltpu.SemaphoreType.DMA((2,)),
        ],
        compiler_params=pltpu.CompilerParams(vmem_limit_bytes=48 * 1024 * 1024),
    )(projected, column_id, row_id, cotangent, embedded, gain, moved, main, rest)


def reduce_kernel(
    grad_ref,
    out_ref,
    twin,
    held,
    across,
    line,
    met,
    tiles,
    total,
    result,
    twin_send,
    twin_recv,
    across_send,
    across_recv,
    line_send,
    line_recv,
    tile_send,
    tile_recv,
    total_send,
    total_recv,
    last_send,
    last_recv,
):
    z, b, x, y, core = place()
    sibling = b + 1 - 2 * core
    first = x * (1 - core) + y * core
    second = y * (1 - core) + x * core

    def chip_of(which, f, s):
        return (s * 4 + f) * (1 - which) + (f * 4 + s) * which

    def target_chip(which, a, half):
        mine = x * (1 - which) + y * which
        f = lax.rem(mine + a, 4)
        return chip_of(which, f, 2 * half + lax.rem(f + which, 2))

    def at(f, s):
        return (z, chip_of(core, f, s) * 2 + core)

    barrier = pltpu.get_barrier_semaphore()
    pl.semaphore_signal(barrier, inc=1, device_id=(z, sibling), device_id_type=MESH)
    for a in range(1, 4):
        pl.semaphore_signal(
            barrier, inc=1, device_id=at(lax.rem(first + a, 4), second), device_id_type=MESH
        )
        pl.semaphore_signal(
            barrier, inc=1, device_id=at(first, lax.rem(second + a, 4)), device_id_type=MESH
        )

    def greet(step, carry):
        pl.semaphore_signal(
            barrier, inc=1, device_id=(lax.rem(z + step, 16), b), device_id_type=MESH
        )
        return carry

    lax.fori_loop(1, 16, greet, 0)
    pl.semaphore_wait(barrier, 22)

    def twin_copy(a, half):
        chip = target_chip(1 - core, a, half)
        return remote(
            grad_ref.at[chip], twin.at[a, half], twin_send.at[a, half], twin_recv.at[a, half], (z, sibling)
        )

    order = (2, 1, 3, 0)
    for a in order:
        for half in range(2):
            twin_copy(a, half).start()

    def across_copy(a):
        return remote(
            held.at[a],
            across.at[a],
            across_send.at[a],
            across_recv.at[a],
            at(lax.rem(first + a, 4), second),
        )

    for a in order:
        for half in range(2):
            twin_copy(a, half).wait_recv()
            chip = target_chip(core, a, half)
            held[a, half] = (
                grad_ref[chip].astype(jnp.float32) + twin[a, half].astype(jnp.float32)
            ).astype(jnp.bfloat16)
        if a > 0:
            across_copy(a).start()
    for a in (1, 3, 2):
        across_copy(a).wait_recv()
    for half in range(2):
        line[half] = (
            held[0, half].astype(jnp.float32)
            + across[1, half].astype(jnp.float32)
            + across[2, half].astype(jnp.float32)
            + across[3, half].astype(jnp.float32)
        ).astype(jnp.bfloat16)

    parity = lax.rem(first + core, 2)
    owner = lax.rem(first + second, 2) == core

    def line_copy(half):
        to = 2 * half + parity
        away = lax.rem(to - second + 4, 4)
        return remote(
            line.at[half],
            met.at[away],
            line_send.at[half],
            line_recv.at[away],
            at(first, to),
        )

    for a in range(1, 4):
        across_copy(a).wait_send()
    for half in range(2):
        to = 2 * half + parity

        @pl.when(to != second)
        def _():
            line_copy(half).start()

    tile = total.shape[1]

    def tile_copy(index):
        to = 2 * index
        return remote(
            result.at[pl.ds(16 * index, 16)],
            tiles.at[z],
            tile_send.at[index],
            tile_recv.at[z],
            (to, b),
        )

    def tile_wait(slot):
        remote(
            result.at[pl.ds(0, 16)], tiles.at[slot], tile_send.at[0], tile_recv.at[slot], (slot, b)
        ).wait_recv()

    def total_copy(to, index):
        return remote(
            total.at[index],
            total.at[index],
            total_send.at[to],
            total_recv.at[index],
            (to, b),
        )

    @pl.when(owner)
    def _():
        mine = line[second // 2].astype(jnp.float32)
        for away in (1, 3, 2):
            remote(
                line.at[0], met.at[away], line_send.at[0], line_recv.at[away], (z, sibling)
            ).wait_recv()
            mine = mine + met[away].astype(jnp.float32)
        result[...] = mine.astype(jnp.bfloat16)
        for index in range(7):

            @pl.when(z != 2 * index)
            def _():
                tile_copy(index).start()

        @pl.when((z < 14) & (lax.rem(z, 2) == 0))
        def _():
            index = z // 2
            tiles[z] = result[pl.ds(pl.multiple_of(16 * index, 16), 16), :]

            def take(step, carry):
                tile_wait(lax.rem(z + step, 16))
                return carry

            lax.fori_loop(1, 16, take, 0)
            value = tiles[0].astype(jnp.float32)
            for slot in range(1, 16):
                value = value + tiles[slot].astype(jnp.float32)
            total[index] = value.astype(jnp.bfloat16)

            def spread(step, carry):
                total_copy(lax.rem(z + step, 16), index).start()
                return carry

            lax.fori_loop(1, 16, spread, 0)

        for index in range(7):

            @pl.when(z != 2 * index)
            def _():
                total_copy(0, index).wait_recv()

        remote(total, total, last_send, last_recv, (z, sibling)).start()

        for index in range(7):

            @pl.when(z != 2 * index)
            def _():
                tile_copy(index).wait_send()

        @pl.when((z < 14) & (lax.rem(z, 2) == 0))
        def _():
            def spent(step, carry):
                total_copy(lax.rem(z + step, 16), z // 2).wait_send()
                return carry

            lax.fori_loop(1, 16, spent, 0)

        remote(total, total, last_send, last_recv, (z, sibling)).wait_send()

    @pl.when(jnp.logical_not(owner))
    def _():
        remote(total, total, last_send, last_recv, (z, sibling)).wait_recv()

    for a in range(4):
        for half in range(2):
            twin_copy(a, half).wait_send()
    for half in range(2):
        to = 2 * half + parity

        @pl.when(to != second)
        def _():
            line_copy(half).wait_send()

    out_ref[...] = total[...]


def reduce_grad(grad):
    vmem = pl.BlockSpec(memory_space=pltpu.VMEM)
    dma = pltpu.SemaphoreType.DMA
    block = (CHIP_ROWS, PIX_PAD)
    return pl.pallas_call(
        reduce_kernel,
        name="reduce_grad",
        out_shape=jax.ShapeDtypeStruct((7, 16, PIX_PAD), jnp.bfloat16),
        in_specs=[vmem],
        out_specs=vmem,
        scratch_shapes=[
            pltpu.VMEM((4, 2) + block, jnp.bfloat16),
            pltpu.VMEM((4, 2) + block, jnp.bfloat16),
            pltpu.VMEM((4, 2) + block, jnp.bfloat16),
            pltpu.VMEM((2,) + block, jnp.bfloat16),
            pltpu.VMEM((4,) + block, jnp.bfloat16),
            pltpu.VMEM((16, 16, PIX_PAD), jnp.bfloat16),
            pltpu.VMEM((7, 16, PIX_PAD), jnp.bfloat16),
            pltpu.VMEM(block, jnp.bfloat16),
            dma((4, 2)),
            dma((4, 2)),
            dma((4,)),
            dma((4,)),
            dma((2,)),
            dma((4,)),
            dma((7,)),
            dma((16,)),
            dma((16,)),
            dma((7,)),
            dma,
            dma,
        ],
        compiler_params=pltpu.CompilerParams(
            collective_id=1, has_side_effects=True, vmem_limit_bytes=40 * 1024 * 1024
        ),
    )(grad)


def per_device(
    pixels,
    latent,
    quant_scale,
    embed_bias,
    ln_gain,
    ln_bias,
    qkv_weight,
    cotangent,
    image_length,
    image_source,
    image_target,
):
    member = lax.axis_index("bal")
    members = lax.axis_size("bal")
    length, source, target = image_length[0], image_source[0], image_target[0]
    moving = (target != source) & (length > 0)
    receivers = jnp.arange(members, dtype=jnp.int32)[:, None]
    sender = jnp.sum(
        jnp.where((target[None, :] == receivers) & moving[None, :], source[None, :], 0), axis=1
    )
    gain = ln_gain[None, :]
    main, rest, moved, embedded, projected, column_id, row_id = gather_project(
        qkv_weight.T,
        latent.T,
        quant_scale[None, :],
        embed_bias[None, :],
        gain,
        ln_bias[None, :],
        pixels,
        image_length,
        image_source,
        image_target,
        sender,
    )
    attended, grad = attend(
        projected, column_id, row_id, cotangent, embedded, gain, moved, main, rest
    )
    row_share = D // members
    row_start = member * row_share
    scale_rows = lax.dynamic_slice_in_dim(quant_scale, row_start, row_share, 0)[:, None]
    latent_rows = lax.dynamic_slice_in_dim(latent, row_start, row_share, 0)
    ratio = latent_rows.astype(jnp.float32) / scale_rows
    level = jnp.floor(ratio + 0.5)
    inside = (level >= -8.0) & (level <= 7.0)
    slope = jnp.where(inside, level - ratio, jnp.clip(level, -8.0, 7.0))
    reduced = reduce_grad(grad).reshape(CHIP_ROWS, PIX_PAD)
    summed = lax.dynamic_slice_in_dim(reduced, lax.rem(member, 2) * row_share, row_share, 0)
    summed = summed[:, :PIX].astype(jnp.float32)
    grad_latent = jnp.where(inside, summed, 0.0)
    grad_scale = (1.0 / math.sqrt(PIX * 7.0)) * jnp.sum(summed * slope, axis=1)
    return (attended, grad_latent, grad_scale)


def solution(mesh):
    placed = (
        P(("dp", "bal"), None),
        P(),
        P(),
        P(),
        P(),
        P(),
        P(None, "dp"),
        P(("dp", "bal"), None),
        P("dp", None),
        P("dp", None),
        P("dp", None),
    )
    return jax.shard_map(
        per_device,
        mesh=mesh,
        in_specs=placed,
        out_specs=(P(("dp", "bal"), None), P("bal", None), P("bal")),
        check_vma=False,
    )
```

time: 179 us -> 144 us (0.80)
  matrix products: 43.2 us -> 0 us
  Pallas kernels: 111 us -> 129 us
  other arithmetic: 10.5 us -> 2.9 us
  local copies, waits for them, and re-layouts: 12.7 us -> 10.4 us
    dot_general x14 -> x0, matrix products: 43.2 us -> none  [the longest x1 5.69 us: forward_backward(): jnp.einsum('hqk,qhd->khd', grad_score, queries, preferred_element_type=jn...]
    pallas_call x1 -> x2, Pallas kernels: 68.9 us -> 85.4 us  [the longest x1 68.8 us: gather_project(): pl.pallas_call(gather_kernel, name='gather_project', out_shape=(shape((16...]
    unnamed x59 -> x15, local copies, waits for them, and re-layouts: 12.4 us -> 5.77 us
    broadcast_in_dim x0 -> x4, local copies, waits for them, and re-layouts: none -> 2.81 us  [the longest x1 0.7 us: per_device(): quant_scale[None, :]]
    reduce_sum x5 -> x1, other arithmetic: 3.1 us -> 0.9 us  [per_device(): grad_scale = 1.0 / math.sqrt(PIX * 7.0) * jnp.sum(summed * slope, axis=1)]
    and x2 -> x0, other arithmetic: 2.1 us -> none  [the longest x1 1.96 us: quantize(): inside = (level >= -8.0) & (level <= 7.0)]
    pallas_call x1, Pallas kernels: 41.8 us -> 43.7 us  [reduce_grad(): pl.pallas_call(reduce_kernel, name='reduce_grad', out_shape=jax.ShapeDtyp...]
    dynamic_slice x0 -> x2, local copies, waits for them, and re-layouts: none -> 1.86 us  [the longest x1 1.08 us: per_device(): latent_rows = lax.dynamic_slice_in_dim(latent, row_start, row_share, 0)]
where the time goes in v2:
time: 144 us; the launch traced here: 143 us
  Pallas kernels  129 us (90%)
  local copies, waits for them, and re-layouts  10.4 us (7%)
  other arithmetic  2.9 us (2%)
    pallas_call x1, Pallas kernels, gather_project(): pl.pallas_call(gather_kernel, name='gather_project', out_shape=(shape((16...  68.8 us
    pallas_call x1, Pallas kernels, reduce_grad(): pl.pallas_call(reduce_kernel, name='reduce_grad', out_shape=jax.ShapeDtyp...  43.7 us
    pallas_call x1, Pallas kernels, attend(): pl.pallas_call(attention_kernel, name='attend', out_shape=(shape((rows, H...  16.6 us
    unnamed x15, local copies, waits for them, and re-layouts  5.77 us

profile of v2, /device:TPU:1, one launch (start us, length us, event | category | flops | bytes accessed | tf_op | source)
XLA Modules:
  0.0 143.1 jit_solution(17850724905652619763)
XLA Ops:
  0.6 0.7 broadcast_in_dim.33.scale_ref
  1.3 0.7 broadcast_in_dim.34.bias_ref
  2.0 0.7 broadcast_in_dim.35.gain_ref
  2.7 0.7 broadcast_in_dim.36.shift_ref
  3.4 0.7 and_bitcast_fusion
  4.1 0.8 select_reduce_fusion.sender_ref
  4.9 0.0 copy-start
  4.9 1.6 %copy-done = bf16[1792,588]{0,1:T(8,128)(2,1)S(1)} copy-done((bf16[1792,588]{0,1:T(8,128)(2,1)S(1)}, bf16[1792,588]{0,1:T(8,128)(2,1)}, u32[]{:S(2)}) %copy-start) | copy-done | bytes 2107416
  6.5 0.0 copy-start.1
  6.5 1.1 copy-done.1
  7.6 0.0 copy-start.3
  7.6 1.0 copy-done.3
  8.6 0.7 copy-done.4
  9.3 0.7 copy-done.5
  9.9 0.7 copy-done.6
  10.6 68.8 %gather_project.1 = (bf16[16,128,1792]{2,1,0:T(8,128)(2,1)}, bf16[768,1792]{1,0:T(8,128)(2,1)}, bf16[256,640]{1,0:T(8,128)(2,1)S(1)}, bf16[256,1792]{1,0:T(8,128...) custom-call(bf16[168,1792]{1,0:T(8,128)(2,1)S(1)} %bitcast.8, ...), custom_call_target="tpu_custom_call" | custom-call | tf_op jit(solution)/shard_map/gather_project/pallas_call | solution.py:578
  79.4 0.0 copy-done.2
  79.4 16.6 %attend.1 = (bf16[256,896]{1,0:T(8,128)(2,1)}, bf16[16,112,640]{2,1,0:T(8,128)(2,1)S(1)}) custom-call(bf16[256,2688]{1,0:T(8,128)(2,1)S(1)} %get-tuple-element.12.projected_ref, f32[256,1]{1,0:T(8,128)S(1)} %get-tuple-element.13.column_id_ref, f32[1,256]{1,0:T(1,128)S(1)} %get-tuple-element.14.row_id_ref, bf16[256,896]{1,0:T(8,128)(2,1)S(1)} %copy-done.2, ...), custom_call_target="tpu_custom_call" | custom-call | tf_op jit(solution)/shard_map/attend/pallas_call | solution.py:757
  96.0 1.1 constant_dynamic-slice_fusion
  97.0 0.1 copy.16
  97.2 0.8 dynamic_slice.10
  98.0 43.7 %reduce_grad.1 = bf16[7,16,640]{2,1,0:T(8,128)(2,1)S(1)} custom-call(bf16[16,112,640]{2,1,0:T(8,128)(2,1)S(1)} %get-tuple-element.20.grad_ref), custom_call_target="tpu_custom_call" | custom-call | tf_op jit(solution)/shard_map/reduce_grad/pallas_call | solution.py:1010
  141.7 0.9 fusion
  142.6 0.5 broadcast_multiply_fusion
  (4 shorter events, 0.0 us)
Async XLA Ops:
  4.9 1.6 %copy-start = (bf16[1792,588]{0,1:T(8,128)(2,1)S(1)}, bf16[1792,588]{0,1:T(8,128)(2,1)}, u32[]{:S(2)}) copy-start(bf16[1792,588]{0,1:T(8,128)(2,1)} %param.12) | copy-start | bytes 6322180
  6.5 1.1 copy-start.1
  7.6 1.0 copy-start.3
  8.6 0.7 copy-start.4
  9.3 0.7 copy-start.5
  9.9 0.7 copy-start.6
  10.6 68.8 %copy-start.2 = (bf16[256,896]{1,0:T(8,128)(2,1)S(1)}, bf16[256,896]{1,0:T(8,128)(2,1)}, u32[]{:S(2)}) copy-start(bf16[256,896]{1,0:T(8,128)(2,1)} %cotangent_ref.1) | copy-start | bytes 1376260

commit v3 on v2

--- a/solution.py
+++ b/solution.py
@@ -38,20 +38,30 @@
     return copy
 
 
-def gather_kernel(
-    w_ref,
-    latent_ref,
-    scale_ref,
-    bias_ref,
-    gain_ref,
-    shift_ref,
-    pixels_ref,
+def whole_kernel(
+    weight_in,
+    latent_in,
+    scale_in,
+    bias_in,
+    gain_in,
+    shift_in,
+    pixels_in,
+    cotangent_in,
     length_ref,
     source_ref,
     target_ref,
+    attended_ref,
+    latent_out,
+    scale_out,
+    w_ref,
+    latent_ref,
+    vectors,
+    pixels_ref,
+    cotangent_ref,
+    sender_vector,
     sender_ref,
-    main_out,
-    rest_out,
+    slope,
+    within,
     moved_ref,
     embedded_ref,
     projected_ref,
@@ -68,6 +78,24 @@
     normed,
     part_main,
     part_rest,
+    grad_out,
+    attended,
+    grad_projected,
+    grad_main,
+    grad_rest,
+    grad_normed,
+    grad_embedded,
+    grad_ref,
+    twin,
+    held,
+    across,
+    line,
+    met,
+    tiles,
+    total,
+    summed,
+    final,
+    load_sem,
     z_send,
     z_recv,
     ring_send,
@@ -82,7 +110,18 @@
     plane_recv,
     pair_send,
     pair_recv,
-    save_sem,
+    twin_send,
+    twin_recv,
+    across_send,
+    across_recv,
+    line_send,
+    line_recv,
+    tile_send,
+    tile_recv,
+    total_send,
+    total_recv,
+    last_send,
+    last_recv,
 ):
     z, b, x, y, core = place()
     sibling = b + 1 - 2 * core
@@ -102,6 +141,22 @@
         )
         return carry
 
+    loads = []
+    for index, (source, held_at) in enumerate(
+        (
+            (weight_in, w_ref),
+            (pixels_in, pixels_ref),
+            (latent_in, latent_ref),
+            (scale_in, vectors.at[0]),
+            (bias_in, vectors.at[1]),
+            (gain_in, vectors.at[2]),
+            (shift_in, vectors.at[3]),
+            (cotangent_in, cotangent_ref),
+        )
+    ):
+        loads.append(pltpu.make_async_copy(source, held_at, load_sem.at[index]))
+        loads[-1].start()
+    scale_ref, bias_ref, gain_ref, shift_ref = (vectors.at[pl.ds(i, 1)] for i in range(4))
     lax.fori_loop(1, 16, greet_line, 0)
     lax.fori_loop(1, 32, greet_plane, 0)
 
@@ -110,6 +165,8 @@
 
     def slice_lanes(where):
         return pl.ds(pl.multiple_of(lax.rem(where, 2) * 896, 128), 896)
+
+    loads[0].wait()
 
     @pl.when(core == 0)
     def _():
@@ -231,6 +288,14 @@
     leaving_any = jnp.sum(jnp.where(leaving, 1.0, 0.0), axis=1, keepdims=True)
     leaving_row = jnp.where(leaving_any > 0.0, leaving_row, -1.0)
     count_in = pixels_ref.shape[0]
+    whole_col = [turned(ref[...]) for ref in (length_ref, source_ref, target_ref)]
+    senders = jnp.where(
+        (whole_col[2] == along) & (whole_col[2] != whole_col[1]) & (whole_col[0] > 0), whole_col[1], 0
+    )
+    sender_vector[...] = jnp.sum(senders, axis=0, keepdims=True)
+    load_sender = pltpu.make_async_copy(sender_vector, sender_ref, load_sem.at[8])
+    load_sender.start()
+    loads[1].wait()
     rows_in[:, pl.ds(512, 128)] = jnp.zeros((rows_in.shape[0], 128), jnp.bfloat16)
     rows_in[pl.ds(0, count_in), pl.ds(0, PIX)] = pixels_ref[...]
     picks = lax.broadcasted_iota(jnp.int32, (MOVE_ROWS, count_in), 1).astype(jnp.float32)
@@ -395,6 +460,7 @@
 
     chunk_start(0)
     ring_step(1)
+    load_sender.wait()
 
     @pl.when(b < PIECES)
     def _():
@@ -405,11 +471,11 @@
             return carry
 
         lax.fori_loop(1, 32, take, 0)
-        arrived[b] = inbox[sender_ref[b]]
+        arrived[b] = inbox[jnp.clip(sender_ref[0, b], 0, 31)]
 
         def send_back(step, carry):
             target = lax.rem(b + step, 32)
-            stage[target] = inbox[sender_ref[target]]
+            stage[target] = inbox[jnp.clip(sender_ref[0, target], 0, 31)]
             back_copy(target, b).start()
             return carry
 
@@ -418,7 +484,18 @@
     chunk_first(0)
     ring_step(2)
     quant[pl.ds(576, 64), :] = jnp.zeros((64, D), jnp.bfloat16)
+    for index in range(2, 7):
+        loads[index].wait()
     lax.fori_loop(0, 7, quantize_part, 0)
+    share = D // 32
+    window = jnp.minimum(chip * CHIP_ROWS // 128 * 128, D - 256)
+    lanes = pl.ds(pl.multiple_of(window, 128), 256)
+    ratio = latent_ref[:, lanes].astype(jnp.float32) / scale_ref[:, lanes]
+    level = jnp.floor(ratio + 0.5)
+    inside = (level >= -8.0) & (level <= 7.0)
+    slope[...] = jnp.where(inside, level - ratio, jnp.clip(level, -8.0, 7.0)).T
+    within[...] = jnp.where(inside, 1.0, 0.0).T
+    share_rows = pl.ds(pl.multiple_of(chip * CHIP_ROWS - window + core * share, 8), share)
     chunk_far(0)
     chunk_second(0, 0)
     ring_step(3)
@@ -433,11 +510,11 @@
     image = jnp.sum(jnp.where(covers, entry, 0.0), axis=1, keepdims=True)
     wanted = jnp.where(image > 0.0, wanted, -1.0)
     column_id_ref[...] = image
-    across = lax.broadcasted_iota(jnp.int32, (entries, moved_ref.shape[0]), 1).astype(jnp.float32)
+    row_lane = lax.broadcasted_iota(jnp.int32, (entries, moved_ref.shape[0]), 1).astype(jnp.float32)
     covers_turned = (
         (target_col[:, :1] == member)
-        & (across >= target_start_col)
-        & (across < target_start_col + length_col[:, :1])
+        & (row_lane >= target_start_col)
+        & (row_lane < target_start_col + length_col[:, :1])
     )
     entry_down = (lax.broadcasted_iota(jnp.int32, (entries, 1), 0) + 1).astype(jnp.float32)
     row_id_ref[...] = jnp.sum(jnp.where(covers_turned, entry_down, 0.0), axis=0, keepdims=True)
@@ -505,14 +582,10 @@
     project(1 - core, 0)
     project(core, 1)
     pair_wait(1)
-    save_main = pltpu.make_async_copy(main, main_out, save_sem.at[0])
-    save_main.start()
     project(1 - core, 1)
     for way in range(2):
         for step in range(1, last[way] + 1):
             hand_copy(1 - core, way, step).wait_recv()
-    save_rest = pltpu.make_async_copy(rest, rest_out, save_sem.at[1])
-    save_rest.start()
     for part in range(3):
         part_rest[:, 256 * part : 256 * part + 256] = lax.dot_general(
             normed[...],
@@ -526,130 +599,7 @@
         joined.append(part_rest[:, REST_PAD * plane : REST_PAD * plane + SHARD - MAIN])
     projected_ref[...] = jnp.concatenate(joined, axis=1)
 
-    for step in range(1, 16):
-
-        @pl.when(z_mine(step))
-        def _():
-            z_copy(step).wait_send()
-
-    for way in range(2):
-        for step in range(1, last[way] + 1):
-            for part in range(2):
-                ring_copy(way, step, part).wait_send()
-            hand_copy(core, way, step).wait_send()
-
-    def sent_out(step, carry):
-        target = lax.rem(b + step, 32)
-
-        @pl.when(target < PIECES)
-        def _():
-            out_copy(target, b).wait_send()
-
-        return carry
-
-    lax.fori_loop(1, 32, sent_out, 0)
-
-    @pl.when(b < PIECES)
-    def _():
-        def sent_back(step, carry):
-            back_copy(lax.rem(b + step, 32), b).wait_send()
-            return carry
-
-        lax.fori_loop(1, 32, sent_back, 0)
-
-    for chunk in range(2):
-        for kind in range(4):
-            first_copy(chunk, kind).wait_send()
-            for index in range(4):
-                second_copy(chunk, index, kind).wait_send()
-        for index in range(4):
-            for second in range(4):
-                pair_copy(core, chunk, index, second).wait_send()
-    save_main.wait()
-    save_rest.wait()
-
-
-def gather_project(weight, latent, scale, bias, gain, shift, pixels, length, source, target, sender):
-    vmem = pl.BlockSpec(memory_space=pltpu.VMEM)
-    anywhere = pl.BlockSpec(memory_space=pl.ANY)
-    dma = pltpu.SemaphoreType.DMA
-    rows = 256
-    shape = jax.ShapeDtypeStruct
-    return pl.pallas_call(
-        gather_kernel,
-        name="gather_project",
-        out_shape=(
-            shape((16, MAIN, D), jnp.bfloat16),
-            shape((16 * REST_PAD, D), jnp.bfloat16),
-            shape((rows, PIX_PAD), jnp.bfloat16),
-            shape((rows, D), jnp.bfloat16),
-            shape((rows, 16 * SHARD), jnp.bfloat16),
-            shape((rows, 1), jnp.float32),
-            shape((1, rows), jnp.float32),
-        ),
-        in_specs=[vmem] * 10 + [pl.BlockSpec(memory_space=pltpu.SMEM)],
-        out_specs=(anywhere, anywhere, vmem, vmem, vmem, vmem, vmem),
-        scratch_shapes=[
-            pltpu.VMEM((16, MAIN, D), jnp.bfloat16),
-            pltpu.VMEM((16 * REST_PAD, D), jnp.bfloat16),
-            pltpu.VMEM((pixels.shape[0] + MOVE_ROWS, PIX_PAD), jnp.bfloat16),
-            pltpu.VMEM((PIECES, 32, 128), jnp.bfloat16),
-            pltpu.VMEM((32, 32, 128), jnp.bfloat16),
-            pltpu.VMEM((32, 32, 128), jnp.bfloat16),
-            pltpu.VMEM((PIECES, 32, 128), jnp.bfloat16),
-            pltpu.VMEM((PIX_PAD, D), jnp.bfloat16),
-            pltpu.VMEM((rows, D), jnp.bfloat16),
-            pltpu.VMEM((8, rows, 256), jnp.bfloat16),
-            pltpu.VMEM((rows, 16 * REST_PAD), jnp.bfloat16),
-            dma((16,)),
-            dma((16,)),
-            dma((2, 9, 2)),
-            dma((2, 9, 2)),
-            dma((2, 9)),
-            dma((2, 9)),
-            dma((32,)),
-            dma((32,)),
-            dma((32,)),
-            dma((32,)),
-            dma((2, 20)),
-            dma((2, 20)),
-            dma((2, 16)),
-            dma((2, 16)),
-            dma((2,)),
-        ],
-        compiler_params=pltpu.CompilerParams(
-            collective_id=0, has_side_effects=True, vmem_limit_bytes=48 * 1024 * 1024
-        ),
-    )(weight, latent, scale, bias, gain, shift, pixels, length, source, target, sender)
-
-
-def attention_kernel(
-    projected_ref,
-    column_id_ref,
-    row_id_ref,
-    cotangent_ref,
-    embedded_ref,
-    gain_ref,
-    moved_ref,
-    main_in,
-    rest_in,
-    attended_ref,
-    grad_ref,
-    main,
-    rest,
-    grad_out,
-    attended,
-    grad_projected,
-    grad_main,
-    grad_rest,
-    grad_normed,
-    grad_embedded,
-    load_sem,
-):
-    load_main = pltpu.make_async_copy(main_in, main, load_sem.at[0])
-    load_rest = pltpu.make_async_copy(rest_in, rest, load_sem.at[1])
-    load_main.start()
-    load_rest.start()
+    loads[7].wait()
     width = HEADS * HEAD
     score_scale = HEAD ** (-0.5)
     grad_factor = 1.0 / math.sqrt(131072.0)
@@ -686,8 +636,8 @@
         keys, values = masked(keys), masked(values)
         scores = dot(queries, keys, by_rows) * score_scale
         exponent = jnp.where(same, jnp.exp(scores), 0.0)
-        total = jnp.sum(exponent, axis=1, keepdims=True)
-        attention = exponent / jnp.where(active, total, 1.0)
+        denominator = jnp.sum(exponent, axis=1, keepdims=True)
+        attention = exponent / jnp.where(active, denominator, 1.0)
         soft = attention.astype(jnp.bfloat16)
         attended[:, start:stop] += dot(soft, values)
         grad_attention = dot(out, values, by_rows)
@@ -711,8 +661,6 @@
         rests.append(pad)
     grad_main[...] = jnp.concatenate(mains, axis=1)
     grad_rest[...] = jnp.concatenate(rests, axis=1)
-    load_main.wait()
-    load_rest.wait()
 
     def back_part(part, carry):
         lanes = pl.ds(pl.multiple_of(part * 256, 128), 256)
@@ -723,7 +671,7 @@
 
     lax.fori_loop(0, 7, back_part, 0)
 
-    def norm_part(part, carry):
+    def back_norm_part(part, carry):
         rows = pl.ds(pl.multiple_of(part * 32, 32), 32)
         values = embedded_ref[rows, :].astype(jnp.float32)
         centered = values - jnp.mean(values, axis=1, keepdims=True)
@@ -741,70 +689,12 @@
         )
         return carry
 
-    lax.fori_loop(0, 8, norm_part, 0)
+    lax.fori_loop(0, 8, back_norm_part, 0)
     for part in range(2):
         block = dot(grad_embedded[:, 896 * part : 896 * part + 896], moved_ref[...], by_columns)
         grad_ref[8 * part : 8 * part + 8] = block.astype(jnp.bfloat16).reshape(
             8, CHIP_ROWS, PIX_PAD
         )
-
-
-def attend(projected, column_id, row_id, cotangent, embedded, gain, moved, main, rest):
-    vmem = pl.BlockSpec(memory_space=pltpu.VMEM)
-    anywhere = pl.BlockSpec(memory_space=pl.ANY)
-    rows = projected.shape[0]
-    shape = jax.ShapeDtypeStruct
-    return pl.pallas_call(
-        attention_kernel,
-        name="attend",
-        out_shape=(
-            shape((rows, HEADS * HEAD), jnp.bfloat16),
-            shape((D // CHIP_ROWS, CHIP_ROWS, PIX_PAD), jnp.bfloat16),
-        ),
-        in_specs=[vmem] * 7 + [anywhere] * 2,
-        out_specs=(vmem, vmem),
-        scratch_shapes=[
-            pltpu.VMEM((16, MAIN, D), jnp.bfloat16),
-            pltpu.VMEM((16 * REST_PAD, D), jnp.bfloat16),
-            pltpu.VMEM((rows, HEADS * HEAD), jnp.bfloat16),
-            pltpu.VMEM((rows, HEADS * HEAD), jnp.float32),
-            pltpu.VMEM((rows, 16 * SHARD), jnp.float32),
-            pltpu.VMEM((rows, 16 * MAIN), jnp.bfloat16),
-            pltpu.VMEM((rows, 16 * REST_PAD), jnp.bfloat16),
-            pltpu.VMEM((rows, D), jnp.float32),
-            pltpu.VMEM((rows, D), jnp.bfloat16),
-            pltpu.SemaphoreType.DMA((2,)),
-        ],
-        compiler_params=pltpu.CompilerParams(vmem_limit_bytes=48 * 1024 * 1024),
-    )(projected, column_id, row_id, cotangent, embedded, gain, moved, main, rest)
-
-
-def reduce_kernel(
-    grad_ref,
-    out_ref,
-    twin,
-    held,
-    across,
-    line,
-    met,
-    tiles,
-    total,
-    result,
-    twin_send,
-    twin_recv,
-    across_send,
-    across_recv,
-    line_send,
-    line_recv,
-    tile_send,
-    tile_recv,
-    total_send,
-    total_recv,
-    last_send,
-    last_recv,
-):
-    z, b, x, y, core = place()
-    sibling = b + 1 - 2 * core
     first = x * (1 - core) + y * core
     second = y * (1 - core) + x * core
 
@@ -818,25 +708,6 @@
 
     def at(f, s):
         return (z, chip_of(core, f, s) * 2 + core)
-
-    barrier = pltpu.get_barrier_semaphore()
-    pl.semaphore_signal(barrier, inc=1, device_id=(z, sibling), device_id_type=MESH)
-    for a in range(1, 4):
-        pl.semaphore_signal(
-            barrier, inc=1, device_id=at(lax.rem(first + a, 4), second), device_id_type=MESH
-        )
-        pl.semaphore_signal(
-            barrier, inc=1, device_id=at(first, lax.rem(second + a, 4)), device_id_type=MESH
-        )
-
-    def greet(step, carry):
-        pl.semaphore_signal(
-            barrier, inc=1, device_id=(lax.rem(z + step, 16), b), device_id_type=MESH
-        )
-        return carry
-
-    lax.fori_loop(1, 16, greet, 0)
-    pl.semaphore_wait(barrier, 22)
 
     def twin_copy(a, half):
         chip = target_chip(1 - core, a, half)
@@ -905,7 +776,7 @@
     def tile_copy(index):
         to = 2 * index
         return remote(
-            result.at[pl.ds(16 * index, 16)],
+            summed.at[pl.ds(16 * index, 16)],
             tiles.at[z],
             tile_send.at[index],
             tile_recv.at[z],
@@ -914,7 +785,7 @@
 
     def tile_wait(slot):
         remote(
-            result.at[pl.ds(0, 16)], tiles.at[slot], tile_send.at[0], tile_recv.at[slot], (slot, b)
+            summed.at[pl.ds(0, 16)], tiles.at[slot], tile_send.at[0], tile_recv.at[slot], (slot, b)
         ).wait_recv()
 
     def total_copy(to, index):
@@ -934,7 +805,7 @@
                 line.at[0], met.at[away], line_send.at[0], line_recv.at[away], (z, sibling)
             ).wait_recv()
             mine = mine + met[away].astype(jnp.float32)
-        result[...] = mine.astype(jnp.bfloat16)
+        summed[...] = mine.astype(jnp.bfloat16)
         for index in range(7):
 
             @pl.when(z != 2 * index)
@@ -944,7 +815,7 @@
         @pl.when((z < 14) & (lax.rem(z, 2) == 0))
         def _():
             index = z // 2
-            tiles[z] = result[pl.ds(pl.multiple_of(16 * index, 16), 16), :]
+            tiles[z] = summed[pl.ds(pl.multiple_of(16 * index, 16), 16), :]
 
             def take(step, carry):
                 tile_wait(lax.rem(z + step, 16))
@@ -1000,20 +871,105 @@
         def _():
             line_copy(half).wait_send()
 
-    out_ref[...] = total[...]
-
-
-def reduce_grad(grad):
+
+    rows = total[...].astype(jnp.float32).reshape(CHIP_ROWS, PIX_PAD)
+    final[...] = rows
+    mine = final[pl.ds(pl.multiple_of(core * share, 8), share), pl.ds(0, PIX)]
+    latent_out[...] = jnp.where(within[share_rows, :] > 0.0, mine, 0.0)
+    scale_out[...] = (1.0 / math.sqrt(PIX * 7.0)) * jnp.sum(mine * slope[share_rows, :], axis=1)
+
+    for step in range(1, 16):
+
+        @pl.when(z_mine(step))
+        def _():
+            z_copy(step).wait_send()
+
+    for way in range(2):
+        for step in range(1, last[way] + 1):
+            for part in range(2):
+                ring_copy(way, step, part).wait_send()
+            hand_copy(core, way, step).wait_send()
+
+    def sent_out(step, carry):
+        target = lax.rem(b + step, 32)
+
+        @pl.when(target < PIECES)
+        def _():
+            out_copy(target, b).wait_send()
+
+        return carry
+
+    lax.fori_loop(1, 32, sent_out, 0)
+
+    @pl.when(b < PIECES)
+    def _():
+        def sent_back(step, carry):
+            back_copy(lax.rem(b + step, 32), b).wait_send()
+            return carry
+
+        lax.fori_loop(1, 32, sent_back, 0)
+
+    for chunk in range(2):
+        for kind in range(4):
+            first_copy(chunk, kind).wait_send()
+            for index in range(4):
+                second_copy(chunk, index, kind).wait_send()
+        for index in range(4):
+            for second in range(4):
+                pair_copy(core, chunk, index, second).wait_send()
+
+
+def whole(weight, latent, scale, bias, gain, shift, pixels, cotangent, length, source, target):
     vmem = pl.BlockSpec(memory_space=pltpu.VMEM)
+    anywhere = pl.BlockSpec(memory_space=pl.ANY)
     dma = pltpu.SemaphoreType.DMA
+    rows = cotangent.shape[0]
     block = (CHIP_ROWS, PIX_PAD)
+    shape = jax.ShapeDtypeStruct
     return pl.pallas_call(
-        reduce_kernel,
-        name="reduce_grad",
-        out_shape=jax.ShapeDtypeStruct((7, 16, PIX_PAD), jnp.bfloat16),
-        in_specs=[vmem],
-        out_specs=vmem,
+        whole_kernel,
+        name="whole",
+        out_shape=(
+            shape((rows, HEADS * HEAD), jnp.bfloat16),
+            shape((D // 32, PIX), jnp.float32),
+            shape((D // 32,), jnp.float32),
+        ),
+        in_specs=[anywhere] * 8 + [vmem] * 3,
+        out_specs=(vmem, vmem, vmem),
         scratch_shapes=[
+            pltpu.VMEM((SHARD, D), jnp.bfloat16),
+            pltpu.VMEM((PIX, D), jnp.bfloat16),
+            pltpu.VMEM((8, D), jnp.float32),
+            pltpu.VMEM(pixels.shape, jnp.bfloat16),
+            pltpu.VMEM(cotangent.shape, jnp.bfloat16),
+            pltpu.VMEM((1, 128), jnp.int32),
+            pltpu.SMEM((1, 128), jnp.int32),
+            pltpu.VMEM((256, PIX), jnp.float32),
+            pltpu.VMEM((256, PIX), jnp.float32),
+            pltpu.VMEM((rows, PIX_PAD), jnp.bfloat16),
+            pltpu.VMEM((rows, D), jnp.bfloat16),
+            pltpu.VMEM((rows, 16 * SHARD), jnp.bfloat16),
+            pltpu.VMEM((rows, 1), jnp.float32),
+            pltpu.VMEM((1, rows), jnp.float32),
+            pltpu.VMEM((16, MAIN, D), jnp.bfloat16),
+            pltpu.VMEM((16 * REST_PAD, D), jnp.bfloat16),
+            pltpu.VMEM((pixels.shape[0] + MOVE_ROWS, PIX_PAD), jnp.bfloat16),
+            pltpu.VMEM((PIECES, 32, 128), jnp.bfloat16),
+            pltpu.VMEM((32, 32, 128), jnp.bfloat16),
+            pltpu.VMEM((32, 32, 128), jnp.bfloat16),
+            pltpu.VMEM((PIECES, 32, 128), jnp.bfloat16),
+            pltpu.VMEM((PIX_PAD, D), jnp.bfloat16),
+            pltpu.VMEM((rows, D), jnp.bfloat16),
+            pltpu.VMEM((8, rows, 256), jnp.bfloat16),
+            pltpu.VMEM((rows, 16 * REST_PAD), jnp.bfloat16),
+            pltpu.VMEM((rows, HEADS * HEAD), jnp.bfloat16),
+            pltpu.VMEM((rows, HEADS * HEAD), jnp.float32),
+            pltpu.VMEM((rows, 16 * SHARD), jnp.float32),
+            pltpu.VMEM((rows, 16 * MAIN), jnp.bfloat16),
+            pltpu.VMEM((rows, 16 * REST_PAD), jnp.bfloat16),
+            pltpu.VMEM((rows, D), jnp.float32),
+            pltpu.VMEM((rows, D), jnp.bfloat16),
+            pltpu.VMEM((D // CHIP_ROWS,) + block, jnp.bfloat16),
             pltpu.VMEM((4, 2) + block, jnp.bfloat16),
             pltpu.VMEM((4, 2) + block, jnp.bfloat16),
             pltpu.VMEM((4, 2) + block, jnp.bfloat16),
@@ -1022,6 +978,22 @@
             pltpu.VMEM((16, 16, PIX_PAD), jnp.bfloat16),
             pltpu.VMEM((7, 16, PIX_PAD), jnp.bfloat16),
             pltpu.VMEM(block, jnp.bfloat16),
+            pltpu.VMEM(block, jnp.float32),
+            dma((9,)),
+            dma((16,)),
+            dma((16,)),
+            dma((2, 9, 2)),
+            dma((2, 9, 2)),
+            dma((2, 9)),
+            dma((2, 9)),
+            dma((32,)),
+            dma((32,)),
+            dma((32,)),
+            dma((32,)),
+            dma((2, 20)),
+            dma((2, 20)),
+            dma((2, 16)),
+            dma((2, 16)),
             dma((4, 2)),
             dma((4, 2)),
             dma((4,)),
@@ -1036,9 +1008,9 @@
             dma,
         ],
         compiler_params=pltpu.CompilerParams(
-            collective_id=1, has_side_effects=True, vmem_limit_bytes=40 * 1024 * 1024
+            collective_id=0, has_side_effects=True, vmem_limit_bytes=58 * 1024 * 1024
         ),
-    )(grad)
+    )(weight, latent, scale, bias, gain, shift, pixels, cotangent, length, source, target)
 
 
 def per_device(
@@ -1054,45 +1026,19 @@
     image_source,
     image_target,
 ):
-    member = lax.axis_index("bal")
-    members = lax.axis_size("bal")
-    length, source, target = image_length[0], image_source[0], image_target[0]
-    moving = (target != source) & (length > 0)
-    receivers = jnp.arange(members, dtype=jnp.int32)[:, None]
-    sender = jnp.sum(
-        jnp.where((target[None, :] == receivers) & moving[None, :], source[None, :], 0), axis=1
-    )
-    gain = ln_gain[None, :]
-    main, rest, moved, embedded, projected, column_id, row_id = gather_project(
+    return whole(
         qkv_weight.T,
         latent.T,
-        quant_scale[None, :],
-        embed_bias[None, :],
-        gain,
-        ln_bias[None, :],
+        quant_scale,
+        embed_bias,
+        ln_gain,
+        ln_bias,
         pixels,
+        cotangent,
         image_length,
         image_source,
         image_target,
-        sender,
     )
-    attended, grad = attend(
-        projected, column_id, row_id, cotangent, embedded, gain, moved, main, rest
-    )
-    row_share = D // members
-    row_start = member * row_share
-    scale_rows = lax.dynamic_slice_in_dim(quant_scale, row_start, row_share, 0)[:, None]
-    latent_rows = lax.dynamic_slice_in_dim(latent, row_start, row_share, 0)
-    ratio = latent_rows.astype(jnp.float32) / scale_rows
-    level = jnp.floor(ratio + 0.5)
-    inside = (level >= -8.0) & (level <= 7.0)
-    slope = jnp.where(inside, level - ratio, jnp.clip(level, -8.0, 7.0))
-    reduced = reduce_grad(grad).reshape(CHIP_ROWS, PIX_PAD)
-    summed = lax.dynamic_slice_in_dim(reduced, lax.rem(member, 2) * row_share, row_share, 0)
-    summed = summed[:, :PIX].astype(jnp.float32)
-    grad_latent = jnp.where(inside, summed, 0.0)
-    grad_scale = (1.0 / math.sqrt(PIX * 7.0)) * jnp.sum(summed * slope, axis=1)
-    return (attended, grad_latent, grad_scale)
 
 
 def solution(mesh):

time: 144 us -> 126 us (0.88)
  Pallas kernels: 129 us -> 121 us
  local copies, waits for them, and re-layouts: 10.4 us -> 4.57 us
  other arithmetic: 2.9 us -> 0 us
    pallas_call x3 -> x1, Pallas kernels: 129 us -> 121 us  [whole(): pl.pallas_call(whole_kernel, name='whole', out_shape=(shape((rows, HEADS...]
    broadcast_in_dim x4 -> x0, local copies, waits for them, and re-layouts: 2.81 us -> none  [the longest x1 0.7 us: per_device(): quant_scale[None, :]]
    dynamic_slice x2 -> x0, local copies, waits for them, and re-layouts: 1.86 us -> none  [the longest x1 1.08 us: per_device(): latent_rows = lax.dynamic_slice_in_dim(latent, row_start, row_share, 0)]
    reduce_sum x2 -> x0, other arithmetic: 1.68 us -> none  [the longest x1 0.9 us: per_device(): grad_scale = 1.0 / math.sqrt(PIX * 7.0) * jnp.sum(summed * slope, axis=1)]
    unnamed x15 -> x3, local copies, waits for them, and re-layouts: 5.77 us -> 4.57 us
where the time goes in v3:
time: 126 us
  Pallas kernels  121 us (96%)
  local copies, waits for them, and re-layouts  4.57 us (4%)
    pallas_call x1, Pallas kernels, whole(): pl.pallas_call(whole_kernel, name='whole', out_shape=(shape((rows, HEADS...  121 us
    unnamed x3, local copies, waits for them, and re-layouts  4.57 us

profile of v3, /device:TPU:1, one launch (start us, length us, event | category | flops | bytes accessed | tf_op | source)
XLA Modules:
  0.0 126.1 jit_solution(11085595898637832908)
XLA Ops:
  0.6 120.9 %whole.1 = (bf16[256,896]{1,0:T(8,128)(2,1)}, f32[56,588]{1,0:T(8,128)}, f32[56]{0:T(128)}) custom-call(bf16[168,1792]{1,0:T(8,128)(2,1)} %bitcast.3, bf16[588,1792]{1,0:T(8,128)(2,1)} %bitcast.2, f32[1792]{0:T(1024)} %scale_in.1, f32[1792]{0:T(1024)} %bias_in.1, f32[1792]{0:T(1024)} %gain_in.1, f32[1792]{0:T(1024)} %shift_in.1, bf16[320,588]{1,0:T(8,128)(2,1)} %pixels_in.1, ...), custom_call_target="tpu_custom_call" | custom-call | tf_op jit(solution)/shard_map/whole/pallas_call | solution.py:929
  121.6 1.8 %copy.17 = bf16[256,896]{1,0:T(8,128)(2,1)} copy(bf16[256,896]{1,0:T(8,128)(2,1)} %get-tuple-element.6) | data formatting | bytes 917504
  123.4 1.6 %copy.18 = f32[56,588]{1,0:T(8,128)} copy(f32[56,588]{1,0:T(8,128)} %get-tuple-element.7) | data formatting | bytes 263424
  125.0 1.2 copy.19

commit v4 on v3

--- a/solution.py
+++ b/solution.py
@@ -120,8 +120,6 @@
     tile_recv,
     total_send,
     total_recv,
-    last_send,
-    last_recv,
 ):
     z, b, x, y, core = place()
     sibling = b + 1 - 2 * core
@@ -138,6 +136,12 @@
     def greet_line(step, carry):
         pl.semaphore_signal(
             barrier, inc=1, device_id=(lax.rem(z + step, 16), b), device_id_type=MESH
+        )
+        return carry
+
+    def greet_other(step, carry):
+        pl.semaphore_signal(
+            barrier, inc=1, device_id=(lax.rem(z + step, 16), sibling), device_id_type=MESH
         )
         return carry
 
@@ -158,6 +162,7 @@
         loads[-1].start()
     scale_ref, bias_ref, gain_ref, shift_ref = (vectors.at[pl.ds(i, 1)] for i in range(4))
     lax.fori_loop(1, 16, greet_line, 0)
+    lax.fori_loop(1, 16, greet_other, 0)
     lax.fori_loop(1, 32, greet_plane, 0)
 
     def slice_rows(where):
@@ -179,7 +184,7 @@
         [w_ref[pl.ds(MAIN, SHARD - MAIN), :], jnp.zeros((REST_PAD - SHARD + MAIN, D), jnp.bfloat16)],
         axis=0,
     )
-    pl.semaphore_wait(barrier, 46)
+    pl.semaphore_wait(barrier, 61)
 
     def z_copy(step):
         to = lax.rem(z + step, 16)
@@ -194,9 +199,16 @@
     def z_mine(step):
         return lax.rem(lax.rem(z + step, 16) // 4 + quad, 2) == core
 
-    for step in (1, 15, 2, 14, 3, 13, 4, 12, 5, 11, 6, 10, 7, 9, 8):
-
-        @pl.when(z_mine(step))
+    steps = (1, 15, 2, 14, 3, 13, 4, 12, 5, 11, 6, 10, 7, 9, 8)
+
+    def z_early(step):
+        to = lax.rem(z + step, 16)
+        base = (to // 4) * (1 - core) + core * (to // 4 + 3 + 2 * (lax.rem(to, 4) // 2))
+        return lax.rem(base, 4) == quad
+
+    for step in steps:
+
+        @pl.when(z_mine(step) & z_early(step))
         def _():
             z_copy(step).start()
 
@@ -236,20 +248,19 @@
         )
 
     last = (8, 7)
-    for part in range(2):
+    for way in range(2):
+        ring_copy(way, 1, 0).start()
+
+    def ring_step(part, step):
         for way in range(2):
-            ring_copy(way, 1, part).start()
-
-    def ring_step(step):
-        for part in range(2):
+            if step <= last[way]:
+                ring_wait(way, step, part)
+                if step < last[way]:
+                    ring_copy(way, step + 1, part).start()
+        if part == 1:
             for way in range(2):
                 if step <= last[way]:
-                    ring_wait(way, step, part)
-                    if step < last[way]:
-                        ring_copy(way, step + 1, part).start()
-        for way in range(2):
-            if step <= last[way]:
-                hand_copy(core, way, step).start()
+                    hand_copy(core, way, step).start()
 
     length_row = length_ref[...].astype(jnp.float32)
     source_row = source_ref[...].astype(jnp.float32)
@@ -329,6 +340,12 @@
 
     lax.fori_loop(1, 32, send_out, 0)
 
+    for step in steps:
+
+        @pl.when(z_mine(step) & jnp.logical_not(z_early(step)))
+        def _():
+            z_copy(step).start()
+
     def quad_of(which, chunk):
         base = quad * (1 - which) + which * (quad + 3 + 2 * (lax.rem(z, 4) // 2))
         return lax.rem(base + 2 * chunk, 4)
@@ -459,7 +476,9 @@
         return carry
 
     chunk_start(0)
-    ring_step(1)
+    for way in range(2):
+        ring_copy(way, 1, 1).start()
+    ring_step(0, 1)
     load_sender.wait()
 
     @pl.when(b < PIECES)
@@ -482,7 +501,8 @@
         lax.fori_loop(1, 32, send_back, 0)
 
     chunk_first(0)
-    ring_step(2)
+    ring_step(1, 1)
+    ring_step(0, 2)
     quant[pl.ds(576, 64), :] = jnp.zeros((64, D), jnp.bfloat16)
     for index in range(2, 7):
         loads[index].wait()
@@ -498,7 +518,8 @@
     share_rows = pl.ds(pl.multiple_of(chip * CHIP_ROWS - window + core * share, 8), share)
     chunk_far(0)
     chunk_second(0, 0)
-    ring_step(3)
+    ring_step(1, 2)
+    ring_step(0, 3)
 
     row = lax.broadcasted_iota(jnp.int32, (moved_ref.shape[0], entries), 0).astype(jnp.float32)
     covers = (target_row == member) & (row >= target_start) & (row < target_start + length_row)
@@ -542,25 +563,31 @@
     ).astype(jnp.bfloat16)
     chunk_second(0, 1)
     chunk_start(1)
-    ring_step(4)
+    ring_step(1, 3)
+    ring_step(0, 4)
     lax.fori_loop(0, 4, embed_part, 0)
     chunk_second(0, 2)
     chunk_first(1)
-    ring_step(5)
+    ring_step(1, 4)
+    ring_step(0, 5)
     lax.fori_loop(4, 7, embed_part, 0)
     chunk_second(0, 3)
     chunk_far(1)
     chunk_second(1, 0)
-    ring_step(6)
+    ring_step(1, 5)
+    ring_step(0, 6)
     lax.fori_loop(0, 4, norm_part, 0)
     chunk_second(1, 1)
-    chunk_second(1, 2)
-    ring_step(7)
-    lax.fori_loop(4, 8, norm_part, 0)
-    chunk_second(1, 3)
     for index in range(4):
         chunk_last(0, index)
-    ring_step(8)
+    ring_step(1, 6)
+    ring_step(0, 7)
+    lax.fori_loop(4, 8, norm_part, 0)
+    chunk_second(1, 2)
+    ring_step(1, 7)
+    ring_step(0, 8)
+    chunk_second(1, 3)
+    ring_step(1, 8)
     for index in range(4):
         chunk_last(1, index)
 
@@ -697,6 +724,7 @@
         )
     first = x * (1 - core) + y * core
     second = y * (1 - core) + x * core
+    parts = ((0, 256), (256, 256), (512, 128))
 
     def chip_of(which, f, s):
         return (s * 4 + f) * (1 - which) + (f * 4 + s) * which
@@ -709,174 +737,208 @@
     def at(f, s):
         return (z, chip_of(core, f, s) * 2 + core)
 
-    def twin_copy(a, half):
-        chip = target_chip(1 - core, a, half)
+    def columns(k):
+        return pl.ds(*parts[k])
+
+    def wide(value):
+        return value.astype(jnp.float32)
+
+    def twin_copy(a, half, k):
         return remote(
-            grad_ref.at[chip], twin.at[a, half], twin_send.at[a, half], twin_recv.at[a, half], (z, sibling)
+            grad_ref.at[target_chip(1 - core, a, half), :, columns(k)],
+            twin.at[a, half, :, columns(k)],
+            twin_send.at[a, half, k],
+            twin_recv.at[a, half, k],
+            (z, sibling),
+        )
+
+    def across_copy(a, k):
+        return remote(
+            held.at[a, :, :, columns(k)],
+            across.at[a, :, :, columns(k)],
+            across_send.at[a, k],
+            across_recv.at[a, k],
+            at(lax.rem(first + a, 4), second),
         )
 
     order = (2, 1, 3, 0)
-    for a in order:
-        for half in range(2):
-            twin_copy(a, half).start()
-
-    def across_copy(a):
-        return remote(
-            held.at[a],
-            across.at[a],
-            across_send.at[a],
-            across_recv.at[a],
-            at(lax.rem(first + a, 4), second),
-        )
-
-    for a in order:
-        for half in range(2):
-            twin_copy(a, half).wait_recv()
-            chip = target_chip(core, a, half)
-            held[a, half] = (
-                grad_ref[chip].astype(jnp.float32) + twin[a, half].astype(jnp.float32)
-            ).astype(jnp.bfloat16)
-        if a > 0:
-            across_copy(a).start()
-    for a in (1, 3, 2):
-        across_copy(a).wait_recv()
-    for half in range(2):
-        line[half] = (
-            held[0, half].astype(jnp.float32)
-            + across[1, half].astype(jnp.float32)
-            + across[2, half].astype(jnp.float32)
-            + across[3, half].astype(jnp.float32)
-        ).astype(jnp.bfloat16)
+    spread = range(len(parts))
+    for k in spread:
+        for a in order:
+            for half in range(2):
+                twin_copy(a, half, k).start()
+    for k in spread:
+        for a in order:
+            for half in range(2):
+                twin_copy(a, half, k).wait_recv()
+                chip_here = target_chip(core, a, half)
+                held[a, half, :, columns(k)] = (
+                    wide(grad_ref[chip_here, :, columns(k)]) + wide(twin[a, half, :, columns(k)])
+                ).astype(jnp.bfloat16)
+            if a > 0:
+                across_copy(a, k).start()
 
     parity = lax.rem(first + core, 2)
     owner = lax.rem(first + second, 2) == core
 
-    def line_copy(half):
+    def line_copy(half, k):
         to = 2 * half + parity
         away = lax.rem(to - second + 4, 4)
         return remote(
-            line.at[half],
-            met.at[away],
-            line_send.at[half],
-            line_recv.at[away],
+            line.at[half, :, columns(k)],
+            met.at[away, :, columns(k)],
+            line_send.at[half, k],
+            line_recv.at[away, k],
             at(first, to),
         )
 
-    for a in range(1, 4):
-        across_copy(a).wait_send()
-    for half in range(2):
-        to = 2 * half + parity
-
-        @pl.when(to != second)
+    for k in spread:
+        for a in (1, 3, 2):
+            across_copy(a, k).wait_recv()
+        for half in range(2):
+            line[half, :, columns(k)] = (
+                wide(held[0, half, :, columns(k)])
+                + wide(across[1, half, :, columns(k)])
+                + wide(across[2, half, :, columns(k)])
+                + wide(across[3, half, :, columns(k)])
+            ).astype(jnp.bfloat16)
+
+            @pl.when(2 * half + parity != second)
+            def _():
+                line_copy(half, k).start()
+
+    def tile_copy(index, k):
+        return remote(
+            summed.at[pl.ds(16 * index, 16), columns(k)],
+            tiles.at[z, :, columns(k)],
+            tile_send.at[index, k],
+            tile_recv.at[z, k],
+            (2 * index, b),
+        )
+
+    for k in spread:
+
+        @pl.when(owner)
         def _():
-            line_copy(half).start()
-
-    tile = total.shape[1]
-
-    def tile_copy(index):
-        to = 2 * index
+            mine = wide(line[second // 2, :, columns(k)])
+            for away in (1, 3, 2):
+                remote(
+                    line.at[0, :, columns(k)],
+                    met.at[away, :, columns(k)],
+                    line_send.at[0, k],
+                    line_recv.at[away, k],
+                    (z, sibling),
+                ).wait_recv()
+                mine = mine + wide(met[away, :, columns(k)])
+            summed[:, columns(k)] = mine.astype(jnp.bfloat16)
+            for index in range(7):
+
+                @pl.when(z != 2 * index)
+                def _():
+                    tile_copy(index, k).start()
+
+    collector = owner & (z < 14) & (lax.rem(z, 2) == 0)
+    tile_index = jnp.minimum(z // 2, 6)
+
+    def total_copy(step, which, k):
         return remote(
-            summed.at[pl.ds(16 * index, 16)],
-            tiles.at[z],
-            tile_send.at[index],
-            tile_recv.at[z],
-            (to, b),
-        )
-
-    def tile_wait(slot):
-        remote(
-            summed.at[pl.ds(0, 16)], tiles.at[slot], tile_send.at[0], tile_recv.at[slot], (slot, b)
-        ).wait_recv()
-
-    def total_copy(to, index):
-        return remote(
-            total.at[index],
-            total.at[index],
-            total_send.at[to],
-            total_recv.at[index],
-            (to, b),
-        )
-
-    @pl.when(owner)
-    def _():
-        mine = line[second // 2].astype(jnp.float32)
-        for away in (1, 3, 2):
-            remote(
-                line.at[0], met.at[away], line_send.at[0], line_recv.at[away], (z, sibling)
-            ).wait_recv()
-            mine = mine + met[away].astype(jnp.float32)
-        summed[...] = mine.astype(jnp.bfloat16)
-        for index in range(7):
-
-            @pl.when(z != 2 * index)
+            total.at[tile_index, :, columns(k)],
+            total.at[tile_index, :, columns(k)],
+            total_send.at[step, which, k],
+            total_recv.at[tile_index, k],
+            (lax.rem(z + step, 16), chip * 2 + which),
+        )
+
+    def total_goes(step, which):
+        wanted_there = (tile_index <= 3) if which == 0 else (tile_index >= 3)
+        return wanted_there & ((step != 0) | (core != which))
+
+    for k in spread:
+
+        @pl.when(collector)
+        def _():
+            tile_rows = pl.ds(pl.multiple_of(16 * tile_index, 16), 16)
+            tiles[z, :, columns(k)] = summed[tile_rows, columns(k)]
+
+            def take(step, carry):
+                slot = lax.rem(z + step, 16)
+                remote(
+                    summed.at[pl.ds(0, 16), columns(k)],
+                    tiles.at[slot, :, columns(k)],
+                    tile_send.at[0, k],
+                    tile_recv.at[slot, k],
+                    (slot, b),
+                ).wait_recv()
+                return carry
+
+            lax.fori_loop(1, 16, take, 0)
+            value = wide(tiles[0, :, columns(k)])
+            for slot in range(1, 16):
+                value = value + wide(tiles[slot, :, columns(k)])
+            total[tile_index, :, columns(k)] = value.astype(jnp.bfloat16)
+
+            def give(step, carry):
+                for which in range(2):
+
+                    @pl.when(total_goes(step, which))
+                    def _():
+                        total_copy(step, which, k).start()
+
+                return carry
+
+            lax.fori_loop(0, 16, give, 0)
+
+    for k in spread:
+        for j in range(4):
+            index = 3 * core + j
+
+            @pl.when(jnp.logical_not(owner & (z == 2 * index)))
             def _():
-                tile_copy(index).start()
-
-        @pl.when((z < 14) & (lax.rem(z, 2) == 0))
-        def _():
-            index = z // 2
-            tiles[z] = summed[pl.ds(pl.multiple_of(16 * index, 16), 16), :]
-
-            def take(step, carry):
-                tile_wait(lax.rem(z + step, 16))
-                return carry
-
-            lax.fori_loop(1, 16, take, 0)
-            value = tiles[0].astype(jnp.float32)
-            for slot in range(1, 16):
-                value = value + tiles[slot].astype(jnp.float32)
-            total[index] = value.astype(jnp.bfloat16)
-
-            def spread(step, carry):
-                total_copy(lax.rem(z + step, 16), index).start()
-                return carry
-
-            lax.fori_loop(1, 16, spread, 0)
-
-        for index in range(7):
-
-            @pl.when(z != 2 * index)
-            def _():
-                total_copy(0, index).wait_recv()
-
-        remote(total, total, last_send, last_recv, (z, sibling)).start()
-
-        for index in range(7):
-
-            @pl.when(z != 2 * index)
-            def _():
-                tile_copy(index).wait_send()
-
-        @pl.when((z < 14) & (lax.rem(z, 2) == 0))
-        def _():
-            def spent(step, carry):
-                total_copy(lax.rem(z + step, 16), z // 2).wait_send()
-                return carry
-
-            lax.fori_loop(1, 16, spent, 0)
-
-        remote(total, total, last_send, last_recv, (z, sibling)).wait_send()
-
-    @pl.when(jnp.logical_not(owner))
-    def _():
-        remote(total, total, last_send, last_recv, (z, sibling)).wait_recv()
-
-    for a in range(4):
-        for half in range(2):
-            twin_copy(a, half).wait_send()
-    for half in range(2):
-        to = 2 * half + parity
-
-        @pl.when(to != second)
-        def _():
-            line_copy(half).wait_send()
-
-
-    rows = total[...].astype(jnp.float32).reshape(CHIP_ROWS, PIX_PAD)
-    final[...] = rows
-    mine = final[pl.ds(pl.multiple_of(core * share, 8), share), pl.ds(0, PIX)]
+                remote(
+                    total.at[index, :, columns(k)],
+                    total.at[index, :, columns(k)],
+                    total_send.at[0, 0, k],
+                    total_recv.at[index, k],
+                    (z, sibling),
+                ).wait_recv()
+
+    final[...] = wide(total[pl.ds(3 * core, 4)]).reshape(64, PIX_PAD)
+    mine = final[pl.ds(pl.multiple_of(core * 8, 8), share), pl.ds(0, PIX)]
     latent_out[...] = jnp.where(within[share_rows, :] > 0.0, mine, 0.0)
     scale_out[...] = (1.0 / math.sqrt(PIX * 7.0)) * jnp.sum(mine * slope[share_rows, :], axis=1)
+
+    for k in spread:
+        for a in range(4):
+            for half in range(2):
+                twin_copy(a, half, k).wait_send()
+            if a > 0:
+                across_copy(a, k).wait_send()
+        for half in range(2):
+
+            @pl.when(2 * half + parity != second)
+            def _():
+                line_copy(half, k).wait_send()
+
+        @pl.when(owner)
+        def _():
+            for index in range(7):
+
+                @pl.when(z != 2 * index)
+                def _():
+                    tile_copy(index, k).wait_send()
+
+        @pl.when(collector)
+        def _():
+            def given(step, carry):
+                for which in range(2):
+
+                    @pl.when(total_goes(step, which))
+                    def _():
+                        total_copy(step, which, k).wait_send()
+
+                return carry
+
+            lax.fori_loop(0, 16, given, 0)
 
     for step in range(1, 16):
 
@@ -917,6 +979,27 @@
         for index in range(4):
             for second in range(4):
                 pair_copy(core, chunk, index, second).wait_send()
+
+
+def deliver_kernel(*refs):
+    sems = refs[-1]
+    copies = [pltpu.make_async_copy(refs[i], refs[3 + i], sems.at[i]) for i in range(3)]
+    for copy in copies:
+        copy.start()
+    for copy in copies:
+        copy.wait()
+
+
+def deliver(*arrays):
+    anywhere = pl.BlockSpec(memory_space=pl.ANY)
+    return pl.pallas_call(
+        deliver_kernel,
+        name="deliver",
+        out_shape=tuple(jax.ShapeDtypeStruct(a.shape, a.dtype) for a in arrays),
+        in_specs=[anywhere] * 3,
+        out_specs=(anywhere,) * 3,
+        scratch_shapes=[pltpu.SemaphoreType.DMA((3,))],
+    )(*arrays)
 
 
 def whole(weight, latent, scale, bias, gain, shift, pixels, cotangent, length, source, target):
@@ -978,7 +1061,7 @@
             pltpu.VMEM((16, 16, PIX_PAD), jnp.bfloat16),
             pltpu.VMEM((7, 16, PIX_PAD), jnp.bfloat16),
             pltpu.VMEM(block, jnp.bfloat16),
-            pltpu.VMEM(block, jnp.float32),
+            pltpu.VMEM((64, PIX_PAD), jnp.float32),
             dma((9,)),
             dma((16,)),
             dma((16,)),
@@ -994,18 +1077,16 @@
             dma((2, 20)),
             dma((2, 16)),
             dma((2, 16)),
-            dma((4, 2)),
-            dma((4, 2)),
-            dma((4,)),
-            dma((4,)),
-            dma((2,)),
-            dma((4,)),
-            dma((7,)),
-            dma((16,)),
-            dma((16,)),
-            dma((7,)),
-            dma,
-            dma,
+            dma((4, 2, 3)),
+            dma((4, 2, 3)),
+            dma((4, 3)),
+            dma((4, 3)),
+            dma((2, 3)),
+            dma((4, 3)),
+            dma((7, 3)),
+            dma((16, 3)),
+            dma((16, 2, 3)),
+            dma((7, 3)),
         ],
         compiler_params=pltpu.CompilerParams(
             collective_id=0, has_side_effects=True, vmem_limit_bytes=58 * 1024 * 1024
@@ -1026,7 +1107,7 @@
     image_source,
     image_target,
 ):
-    return whole(
+    results = whole(
         qkv_weight.T,
         latent.T,
         quant_scale,
@@ -1039,6 +1120,7 @@
         image_source,
         image_target,
     )
+    return deliver(*results)
 
 
 def solution(mesh):

time: 126 us -> 135 us (1.071)
  Pallas kernels: 121 us -> 135 us
  local copies, waits for them, and re-layouts: 4.57 us -> 0 us
    pallas_call x0 -> x1, Pallas kernels: none -> 19.4 us  [deliver(): pl.pallas_call(deliver_kernel, name='deliver', out_shape=tuple((jax.Shape...]
    pallas_call x1, Pallas kernels: 121 us -> 115 us  [whole(): pl.pallas_call(whole_kernel, name='whole', out_shape=(shape((rows, HEADS...]
    unnamed x3 -> x0, local copies, waits for them, and re-layouts: 4.57 us -> none
where the time goes in v4:
time: 135 us
  Pallas kernels  135 us (100%)
    pallas_call x1, Pallas kernels, whole(): pl.pallas_call(whole_kernel, name='whole', out_shape=(shape((rows, HEADS...  115 us
    pallas_call x1, Pallas kernels, deliver(): pl.pallas_call(deliver_kernel, name='deliver', out_shape=tuple((jax.Shape...  19.4 us

profile of v4, /device:TPU:1, one launch (start us, length us, event | category | flops | bytes accessed | tf_op | source)
XLA Modules:
  0.0 135.4 jit_solution(2861882127496555897)
XLA Ops:
  0.6 115.2 %whole.1 = (bf16[256,896]{1,0:T(8,128)(2,1)}, f32[56,588]{1,0:T(8,128)}, f32[56]{0:T(128)}) custom-call(bf16[168,1792]{1,0:T(8,128)(2,1)} %bitcast.3, bf16[588,1792]{1,0:T(8,128)(2,1)} %bitcast.2, f32[1792]{0:T(1024)} %scale_in.1, f32[1792]{0:T(1024)} %bias_in.1, f32[1792]{0:T(1024)} %gain_in.1, f32[1792]{0:T(1024)} %shift_in.1, bf16[320,588]{1,0:T(8,128)(2,1)} %pixels_in.1, ...), custom_call_target="tpu_custom_call" | custom-call | tf_op jit(solution)/shard_map/whole/pallas_call | solution.py:1012
  115.8 19.4 %deliver.1 = (bf16[256,896]{1,0:T(8,128)(2,1)}, f32[56,588]{1,0:T(8,128)}, f32[56]{0:T(128)}) custom-call(bf16[256,896]{1,0:T(8,128)(2,1)} %get-tuple-element.6.refs_0_, f32[56,588]{1,0:T(8,128)} %get-tuple-element.7.refs_1_, f32[56]{0:T(128)} %get-tuple-element.8.refs_2_), custom_call_target="tpu_custom_call" | custom-call | tf_op jit(solution)/shard_map/deliver/pallas_call | solution.py:995

commit v5 on v4

--- a/solution.py
+++ b/solution.py
@@ -775,7 +775,7 @@
                 held[a, half, :, columns(k)] = (
                     wide(grad_ref[chip_here, :, columns(k)]) + wide(twin[a, half, :, columns(k)])
                 ).astype(jnp.bfloat16)
-            if a > 0:
+            if a > 0 and k == 0:
                 across_copy(a, k).start()
 
     parity = lax.rem(first + core, 2)
@@ -793,6 +793,10 @@
         )
 
     for k in spread:
+        for a in (2, 1, 3):
+            across_copy(a, k).wait_send()
+            if k + 1 < len(parts):
+                across_copy(a, k + 1).start()
         for a in (1, 3, 2):
             across_copy(a, k).wait_recv()
         for half in range(2):
@@ -911,8 +915,6 @@
         for a in range(4):
             for half in range(2):
                 twin_copy(a, half, k).wait_send()
-            if a > 0:
-                across_copy(a, k).wait_send()
         for half in range(2):
 
             @pl.when(2 * half + parity != second)
@@ -981,24 +983,20 @@
                 pair_copy(core, chunk, index, second).wait_send()
 
 
-def deliver_kernel(*refs):
-    sems = refs[-1]
-    copies = [pltpu.make_async_copy(refs[i], refs[3 + i], sems.at[i]) for i in range(3)]
-    for copy in copies:
-        copy.start()
-    for copy in copies:
-        copy.wait()
+def deliver_kernel(attended, latent, scale, attended_out, latent_out, scale_out):
+    attended_out[...] = attended[...]
+    latent_out[...] = latent[...]
+    scale_out[...] = scale[...]
 
 
 def deliver(*arrays):
-    anywhere = pl.BlockSpec(memory_space=pl.ANY)
+    vmem = pl.BlockSpec(memory_space=pltpu.VMEM)
     return pl.pallas_call(
         deliver_kernel,
         name="deliver",
         out_shape=tuple(jax.ShapeDtypeStruct(a.shape, a.dtype) for a in arrays),
-        in_specs=[anywhere] * 3,
-        out_specs=(anywhere,) * 3,
-        scratch_shapes=[pltpu.SemaphoreType.DMA((3,))],
+        in_specs=[vmem] * 3,
+        out_specs=(vmem,) * 3,
     )(*arrays)
 
 

time: 135 us -> 117 us (0.87)
  Pallas kernels: 135 us -> 117 us
    pallas_call x1, Pallas kernels: 19.4 us -> 1.93 us  [deliver(): pl.pallas_call(deliver_kernel, name='deliver', out_shape=tuple((jax.Shape...]
where the time goes in v5:
time: 117 us
  Pallas kernels  117 us (100%)
    pallas_call x1, Pallas kernels, whole(): pl.pallas_call(whole_kernel, name='whole', out_shape=(shape((rows, HEADS...  115 us

profile of v5, /device:TPU:1, one launch (start us, length us, event | category | flops | bytes accessed | tf_op | source)
XLA Modules:
  0.0 117.2 jit_solution(15517214510138289780)
XLA Ops:
  0.6 114.6 %whole.1 = (bf16[256,896]{1,0:T(8,128)(2,1)}, f32[56,588]{1,0:T(8,128)}, f32[56]{0:T(128)}) custom-call(bf16[168,1792]{1,0:T(8,128)(2,1)} %bitcast.3, bf16[588,1792]{1,0:T(8,128)(2,1)} %bitcast.2, f32[1792]{0:T(1024)} %scale_in.1, f32[1792]{0:T(1024)} %bias_in.1, f32[1792]{0:T(1024)} %gain_in.1, f32[1792]{0:T(1024)} %shift_in.1, bf16[320,588]{1,0:T(8,128)(2,1)} %pixels_in.1, ...), custom_call_target="tpu_custom_call" | custom-call | tf_op jit(solution)/shard_map/whole/pallas_call | solution.py:1010
  115.2 1.9 %deliver.1 = (bf16[256,896]{1,0:T(8,128)(2,1)}, f32[56,588]{1,0:T(8,128)}, f32[56]{0:T(128)}) custom-call(bf16[256,896]{1,0:T(8,128)(2,1)} %get-tuple-element.6.attended, f32[56,588]{1,0:T(8,128)} %get-tuple-element.7.latent, f32[56]{0:T(128)} %get-tuple-element.8.scale), custom_call_target="tpu_custom_call" | custom-call | tf_op jit(solution)/shard_map/deliver/pallas_call | solution.py:994

commit v6 on v5

--- a/solution.py
+++ b/solution.py
@@ -717,11 +717,6 @@
         return carry
 
     lax.fori_loop(0, 8, back_norm_part, 0)
-    for part in range(2):
-        block = dot(grad_embedded[:, 896 * part : 896 * part + 896], moved_ref[...], by_columns)
-        grad_ref[8 * part : 8 * part + 8] = block.astype(jnp.bfloat16).reshape(
-            8, CHIP_ROWS, PIX_PAD
-        )
     first = x * (1 - core) + y * core
     second = y * (1 - core) + x * core
     parts = ((0, 256), (256, 256), (512, 128))
@@ -764,6 +759,13 @@
     order = (2, 1, 3, 0)
     spread = range(len(parts))
     for k in spread:
+        for part in range(2):
+            block = dot(
+                grad_embedded[:, 896 * part : 896 * part + 896], moved_ref[:, columns(k)], by_columns
+            )
+            grad_ref[8 * part : 8 * part + 8, :, columns(k)] = block.astype(jnp.bfloat16).reshape(
+                8, CHIP_ROWS, parts[k][1]
+            )
         for a in order:
             for half in range(2):
                 twin_copy(a, half, k).start()

time: 117 us -> 118 us (level)
  no operation moved by 1% of the time
where the time goes in v6:
time: 118 us
  Pallas kernels  117 us (99%)
    pallas_call x1, Pallas kernels, whole(): pl.pallas_call(whole_kernel, name='whole', out_shape=(shape((rows, HEADS...  115 us

profile of v6, /device:TPU:1, one launch (start us, length us, event | category | flops | bytes accessed | tf_op | source)
XLA Modules:
  0.0 117.6 jit_solution(2298136533552404501)
XLA Ops:
  0.6 115.0 %whole.1 = (bf16[256,896]{1,0:T(8,128)(2,1)}, f32[56,588]{1,0:T(8,128)}, f32[56]{0:T(128)}) custom-call(bf16[168,1792]{1,0:T(8,128)(2,1)} %bitcast.3, bf16[588,1792]{1,0:T(8,128)(2,1)} %bitcast.2, f32[1792]{0:T(1024)} %scale_in.1, f32[1792]{0:T(1024)} %bias_in.1, f32[1792]{0:T(1024)} %gain_in.1, f32[1792]{0:T(1024)} %shift_in.1, bf16[320,588]{1,0:T(8,128)(2,1)} %pixels_in.1, ...), custom_call_target="tpu_custom_call" | custom-call | tf_op jit(solution)/shard_map/whole/pallas_call | solution.py:1012
  115.7 1.9 %deliver.1 = (bf16[256,896]{1,0:T(8,128)(2,1)}, f32[56,588]{1,0:T(8,128)}, f32[56]{0:T(128)}) custom-call(bf16[256,896]{1,0:T(8,128)(2,1)} %get-tuple-element.6.attended, f32[56,588]{1,0:T(8,128)} %get-tuple-element.7.latent, f32[56]{0:T(128)} %get-tuple-element.8.scale), custom_call_target="tpu_custom_call" | custom-call | tf_op jit(solution)/shard_map/deliver/pallas_call | solution.py:996
